TPU v7x, 32 devices: a whole 2x2x4 slice. The times are simulated.
32 devices in a mesh: dp: 8 (over z, y), seq: 4 (over x, core).
Axes of the slice: x: 2, y: 2, z: 4, core: 2. Of those that a mesh axis runs over, the one named last changes fastest.
Arguments:
- tokens: bfloat16 [16, 576, 768], P('dp', 'seq'), may hold values from -6 to 6
- image_lengths: int32 [16, 4], P('dp'), may hold values from 1 to 573, as said below
- grid_widths: int32 [16, 4], P('dp'), may hold values from 8 to 24
- qkv_weight: bfloat16 [768, 2304], P(('dp', 'seq')), may hold values from -0.21875 to 0.21875
- q_bias: bfloat16 [768], P(('dp', 'seq')), may hold values from -3 to 3
- v_bias: bfloat16 [768], P(('dp', 'seq')), may hold values from -3 to 3
- proj_weight: bfloat16 [768, 768], P(('dp', 'seq')), may hold values from -0.4375 to 0.4375
- proj_bias: bfloat16 [768], P(('dp', 'seq')), may hold values from -2 to 2
- fc1_weight: bfloat16 [768, 3072], P(('dp', 'seq')), may hold values from -0.21875 to 0.21875
- fc1_bias: bfloat16 [3072], P(('dp', 'seq')), may hold values from -3 to 3
- fc2_weight: bfloat16 [3072, 768], P(('dp', 'seq')), may hold values from -0.15625 to 0.15625
- fc2_bias: bfloat16 [768], P(('dp', 'seq')), may hold values from -2 to 2
- norm1_gain: bfloat16 [768], P(('dp', 'seq')), may hold values from 0.099609375 to 1.8984375
- norm1_bias: bfloat16 [768], P(('dp', 'seq')), may hold values from -2 to 2
- norm2_gain: bfloat16 [768], P(('dp', 'seq')), may hold values from 0.099609375 to 1.8984375
- norm2_bias: bfloat16 [768], P(('dp', 'seq')), may hold values from -2 to 2
- scale1: bfloat16 [768], P(('dp', 'seq')), may hold values from 0.099609375 to 1.8984375
- scale2: bfloat16 [768], P(('dp', 'seq')), may hold values from 0.099609375 to 1.8984375
- bias_table: bfloat16 [2209, 12], replicated, may hold values from -5 to 5
- out_grad: bfloat16 [16, 576, 768], P('dp', 'seq'), may hold values from -6 to 6
Outputs:
- mixed: bfloat16 [16, 576, 768], P('dp', 'seq')
- tokens_grad: bfloat16 [16, 576, 768], P('dp', 'seq')
- qkv_weight_grad: float32 [768, 2304], P(('dp', 'seq'))
- q_bias_grad: float32 [768], P(('dp', 'seq'))
- v_bias_grad: float32 [768], P(('dp', 'seq'))
- proj_weight_grad: float32 [768, 768], P(('dp', 'seq'))
- proj_bias_grad: float32 [768], P(('dp', 'seq'))
- fc1_weight_grad: float32 [768, 3072], P(('dp', 'seq'))
- fc1_bias_grad: float32 [3072], P(('dp', 'seq'))
- fc2_weight_grad: float32 [3072, 768], P(('dp', 'seq'))
- fc2_bias_grad: float32 [768], P(('dp', 'seq'))
- norm1_gain_grad: float32 [768], P(('dp', 'seq'))
- norm1_bias_grad: float32 [768], P(('dp', 'seq'))
- norm2_gain_grad: float32 [768], P(('dp', 'seq'))
- norm2_bias_grad: float32 [768], P(('dp', 'seq'))
- scale1_grad: float32 [768], P(('dp', 'seq'))
- scale2_grad: float32 [768], P(('dp', 'seq'))
- table_grad: float32 [2209, 12], replicated
Inputs may be any that keep to these rules, and one draw needn't show every extreme that they name: `image_lengths`: in each row the 4 image lengths sum to at most 576; the rest of the row is padding.
All inputs are finite; a program needn't handle non-finite values.
Results may differ from a plain program's by a relative error of at most 0.014.
Values may be sent and summed in bfloat16 or wider, within the bound.
No kernel may reach another device: no remote copies, remote signals or barrier semaphores. Data moves between devices by JAX's collectives and lax.ppermute only.
A program may use at most 384 MiB of HBM per device.

v0:
```python
import math

import jax
import jax.numpy as jnp
from jax import lax
from jax.sharding import PartitionSpec as P

GRID = 24
ROW_LEN = 576


EPS = 1e-06


def norm_rows(values, gain_vec, offset_vec):
    center = values - jnp.mean(values, axis=-1, keepdims=True)
    spread = jnp.mean(center * center, axis=-1, keepdims=True)
    return center * lax.rsqrt(spread + EPS) * gain_vec + offset_vec


def layout(lengths, widths, row_len):
    end_points = jnp.cumsum(lengths)
    starts = end_points - lengths
    places = jnp.arange(row_len, dtype=jnp.int32)
    segment = jnp.sum((places[:, None] >= end_points[None, :]).astype(jnp.int32), axis=1)
    member = (segment[:, None] == jnp.arange(lengths.shape[0], dtype=jnp.int32)[None, :]).astype(
        jnp.int32
    )
    offset = places - jnp.sum(member * starts[None, :], axis=1)
    across = jnp.sum(member * widths[None, :], axis=1) + (1 - jnp.sum(member, axis=1)) * GRID
    return (segment, offset // across, offset % across)


def pairs(query_side, key_side):
    segment_query, row_query, column_query = query_side
    segment_key, row_key, column_key = key_side
    allowed = segment_query[:, None] == segment_key[None, :]
    row_diff = jnp.clip(row_query[:, None] - row_key[None, :], -(GRID - 1), GRID - 1)
    table_index = (row_diff + GRID - 1) * (2 * GRID - 1) + (
        column_query[:, None] - column_key[None, :] + GRID - 1
    )
    return (allowed, table_index)


def widen(vector):
    return vector.astype(jnp.float32)


def split_heads(block, head_count):
    return block.reshape(block.shape[:2] + (head_count, block.shape[2] // head_count))


def one_hots(table_index, side):
    levels = jnp.arange(side, dtype=jnp.int32)
    rows_hot = ((table_index // side)[..., None] == levels).astype(jnp.bfloat16)
    cols_hot = ((table_index % side)[..., None] == levels).astype(jnp.bfloat16)
    return (rows_hot, cols_hot)


def bias_offsets(hots, table_cube):
    rows_hot, cols_hot = hots
    per_head = []
    for head in range(table_cube.shape[2]):
        inner = jnp.einsum(
            "rqkb,ab->rqka", cols_hot, table_cube[:, :, head], preferred_element_type=jnp.float32
        )
        per_head.append(jnp.sum(rows_hot.astype(jnp.float32) * inner, axis=-1))
    return jnp.stack(per_head, axis=1)


def score_block(query_block, keys_block, query_part, key_part, table_cube):
    allowed, table_index = jax.vmap(pairs)(query_part, key_part)
    head_count = table_cube.shape[2]
    hots = one_hots(table_index, table_cube.shape[0])
    query_heads = split_heads(query_block, head_count)
    key_heads = split_heads(keys_block, head_count)
    product = jnp.einsum(
        "rqhd,rkhd->rhqk", query_heads, key_heads, preferred_element_type=jnp.float32
    )
    offsets = bias_offsets(hots, table_cube)
    scores = jnp.where(allowed[:, None], product + offsets, -1e30)
    return (scores, hots, query_heads, key_heads)


def attention_grads(
    query_block,
    keys_block,
    values_block,
    query_part,
    key_part,
    log_part,
    grad_part,
    table_cube,
    delta_part,
):
    head_count = table_cube.shape[2]
    scores, hots, query_heads, key_heads = score_block(
        query_block, keys_block, query_part, key_part, table_cube
    )
    attention = jnp.exp(scores - log_part)
    grad_heads = split_heads(grad_part, head_count)
    grad_attention = jnp.einsum(
        "rqhd,rkhd->rhqk",
        grad_heads,
        split_heads(values_block, head_count),
        preferred_element_type=jnp.float32,
    )
    delta_part = jnp.sum(attention * grad_attention, axis=-1, keepdims=True)
    grad_scores = (attention * (grad_attention - delta_part)).astype(jnp.bfloat16)
    return (attention, grad_scores, grad_heads, query_heads, key_heads, hots, delta_part)


def table_sum(grad_scores, hots, table_cube):
    rows_hot, cols_hot = hots
    side = table_cube.shape[0]
    per_head = []
    for head in range(table_cube.shape[2]):
        weighted = cols_hot * grad_scores[:, head][..., None]
        per_head.append(
            jnp.einsum("rqka,rqkb->ab", rows_hot, weighted, preferred_element_type=jnp.float32)
        )
    return jnp.stack(per_head, axis=-1).reshape(side * side, table_cube.shape[2])


def local(
    tokens,
    image_lengths,
    grid_widths,
    qkv_weight,
    q_bias,
    v_bias,
    proj_weight,
    proj_bias,
    fc1_weight,
    fc1_bias,
    fc2_weight,
    fc2_bias,
    norm1_gain,
    norm1_bias,
    norm2_gain,
    norm2_bias,
    scale1,
    scale2,
    bias_table,
    out_grad,
):
    gathered = (
        lax.all_gather(qkv_weight, ("dp", "seq"), axis=0, tiled=True),
        lax.all_gather(q_bias, ("dp", "seq"), axis=0, tiled=True),
        lax.all_gather(v_bias, ("dp", "seq"), axis=0, tiled=True),
        lax.all_gather(proj_weight, ("dp", "seq"), axis=0, tiled=True),
        lax.all_gather(proj_bias, ("dp", "seq"), axis=0, tiled=True),
        lax.all_gather(fc1_weight, ("dp", "seq"), axis=0, tiled=True),
        lax.all_gather(fc1_bias, ("dp", "seq"), axis=0, tiled=True),
        lax.all_gather(fc2_weight, ("dp", "seq"), axis=0, tiled=True),
        lax.all_gather(fc2_bias, ("dp", "seq"), axis=0, tiled=True),
        lax.all_gather(norm1_gain, ("dp", "seq"), axis=0, tiled=True),
        lax.all_gather(norm1_bias, ("dp", "seq"), axis=0, tiled=True),
        lax.all_gather(norm2_gain, ("dp", "seq"), axis=0, tiled=True),
        lax.all_gather(norm2_bias, ("dp", "seq"), axis=0, tiled=True),
        lax.all_gather(scale1, ("dp", "seq"), axis=0, tiled=True),
        lax.all_gather(scale2, ("dp", "seq"), axis=0, tiled=True),
    )
    (
        w_qkv,
        b_query,
        b_value,
        w_proj,
        b_proj,
        w_up,
        b_up,
        w_down,
        b_down,
        gain_one,
        shift_one,
        gain_two,
        shift_two,
        layer_one,
        layer_two,
    ) = gathered
    row_count, shard_len, model_width = tokens.shape
    head_count = bias_table.shape[1]
    query_scale = (model_width // head_count) ** (-0.5)
    side = 2 * GRID - 1
    table_cube = bias_table.reshape(side, side, head_count)
    group_size = math.gcd(row_count, 4)

    def grouped(array):
        return array.reshape((row_count // group_size, group_size) + array.shape[1:])

    def ungrouped(array):
        return array.reshape((row_count,) + array.shape[2:])

    full_side = jax.vmap(lambda lengths, widths: layout(lengths, widths, ROW_LEN))(
        image_lengths, grid_widths
    )
    seq_first = lax.axis_index("seq") * shard_len
    query_side = tuple(
        (lax.dynamic_slice_in_dim(member, seq_first, shard_len, 1) for member in full_side)
    )
    side_groups = tuple((grouped(member) for member in query_side))
    full_groups = tuple((grouped(member) for member in full_side))
    inputs = tokens.astype(jnp.float32)
    normed, norm_one_pull = jax.vjp(norm_rows, inputs, widen(gain_one), widen(shift_one))
    normed_low = normed.astype(jnp.bfloat16)
    joint_qkv = jnp.einsum("rtd,de->rte", normed_low, w_qkv, preferred_element_type=jnp.float32)
    queries = ((joint_qkv[..., :model_width] + widen(b_query)) * query_scale).astype(jnp.bfloat16)
    key_rows = joint_qkv[..., model_width : 2 * model_width].astype(jnp.bfloat16)
    value_rows = (joint_qkv[..., 2 * model_width :] + widen(b_value)).astype(jnp.bfloat16)
    keys_all, values_all = (
        lax.all_gather(key_rows, "seq", axis=1, tiled=True),
        lax.all_gather(value_rows, "seq", axis=1, tiled=True),
    )

    def forward_block(block_in):
        query_block, keys_block, values_block, query_part, key_part = block_in
        scores, hots, query_heads, key_heads = score_block(
            query_block, keys_block, query_part, key_part, table_cube
        )
        highest = jnp.max(scores, axis=-1, keepdims=True)
        raised = jnp.exp(scores - highest)
        denominator = jnp.sum(raised, axis=-1, keepdims=True)
        attention = (raised / denominator).astype(jnp.bfloat16)
        heads_out = jnp.einsum(
            "rhqk,rkhd->rqhd",
            attention,
            split_heads(values_block, head_count),
            preferred_element_type=jnp.float32,
        )
        return (
            heads_out.reshape(query_block.shape).astype(jnp.bfloat16),
            highest + jnp.log(denominator),
        )

    joined_groups, log_total = lax.map(
        forward_block,
        (grouped(queries), grouped(keys_all), grouped(values_all), side_groups, full_groups),
    )
    joined = ungrouped(joined_groups)
    branch = jnp.einsum("rtd,de->rte", joined, w_proj, preferred_element_type=jnp.float32) + widen(
        b_proj
    )
    middle = inputs + widen(layer_one) * branch
    normed_two, norm_two_pull = jax.vjp(norm_rows, middle, widen(gain_two), widen(shift_two))
    low_two = normed_two.astype(jnp.bfloat16)
    before = jnp.einsum("rtd,df->rtf", low_two, w_up, preferred_element_type=jnp.float32) + widen(
        b_up
    )
    activated, gelu_pull = jax.vjp(lambda hidden: jax.nn.gelu(hidden, approximate=False), before)
    act_low = activated.astype(jnp.bfloat16)
    down_out = jnp.einsum(
        "rtf,fd->rtd", act_low, w_down, preferred_element_type=jnp.float32
    ) + widen(b_down)
    mixed = (middle + widen(layer_two) * down_out).astype(jnp.bfloat16)
    regained = (
        lax.all_gather(qkv_weight, ("dp", "seq"), axis=0, tiled=True),
        lax.all_gather(q_bias, ("dp", "seq"), axis=0, tiled=True),
        lax.all_gather(v_bias, ("dp", "seq"), axis=0, tiled=True),
        lax.all_gather(proj_weight, ("dp", "seq"), axis=0, tiled=True),
        lax.all_gather(proj_bias, ("dp", "seq"), axis=0, tiled=True),
        lax.all_gather(fc1_weight, ("dp", "seq"), axis=0, tiled=True),
        lax.all_gather(fc1_bias, ("dp", "seq"), axis=0, tiled=True),
        lax.all_gather(fc2_weight, ("dp", "seq"), axis=0, tiled=True),
        lax.all_gather(fc2_bias, ("dp", "seq"), axis=0, tiled=True),
        lax.all_gather(norm1_gain, ("dp", "seq"), axis=0, tiled=True),
        lax.all_gather(norm1_bias, ("dp", "seq"), axis=0, tiled=True),
        lax.all_gather(norm2_gain, ("dp", "seq"), axis=0, tiled=True),
        lax.all_gather(norm2_bias, ("dp", "seq"), axis=0, tiled=True),
        lax.all_gather(scale1, ("dp", "seq"), axis=0, tiled=True),
        lax.all_gather(scale2, ("dp", "seq"), axis=0, tiled=True),
    )
    (
        w_qkv,
        b_query,
        b_value,
        w_proj,
        b_proj,
        w_up,
        b_up,
        w_down,
        b_down,
        gain_one,
        shift_one,
        gain_two,
        shift_two,
        layer_one,
        layer_two,
    ) = regained
    upstream = out_grad.astype(jnp.float32)
    grad_layer_two = jnp.sum(upstream * down_out, axis=(0, 1))
    grad_after = (widen(layer_two) * upstream).astype(jnp.bfloat16)
    grad_b_down = jnp.sum(grad_after.astype(jnp.float32), axis=(0, 1))
    grad_w_down = jnp.einsum("rtf,rtd->fd", act_low, grad_after, preferred_element_type=jnp.float32)
    grad_act = jnp.einsum("rtd,fd->rtf", grad_after, w_down, preferred_element_type=jnp.float32)
    grad_before = gelu_pull(grad_act)[0].astype(jnp.bfloat16)
    grad_b_up = jnp.sum(grad_before.astype(jnp.float32), axis=(0, 1))
    grad_w_up = jnp.einsum("rtd,rtf->df", low_two, grad_before, preferred_element_type=jnp.float32)
    grad_low_two = jnp.einsum("rtf,df->rtd", grad_before, w_up, preferred_element_type=jnp.float32)
    grad_middle_in, grad_gain_two, grad_shift_two = norm_two_pull(grad_low_two)
    grad_middle = upstream + grad_middle_in
    grad_layer_one = jnp.sum(grad_middle * branch, axis=(0, 1))
    grad_branch = (widen(layer_one) * grad_middle).astype(jnp.bfloat16)
    grad_b_proj = jnp.sum(grad_branch.astype(jnp.float32), axis=(0, 1))
    grad_w_proj = jnp.einsum("rtd,rte->de", joined, grad_branch, preferred_element_type=jnp.float32)
    grad_joined = jnp.einsum(
        "rte,de->rtd", grad_branch, w_proj, preferred_element_type=jnp.float32
    ).astype(jnp.bfloat16)

    def backward_block(block_in):
        query_block, keys_block, values_block, query_part, key_part, log_part, grad_part = block_in
        attention, grad_scores, grad_heads, query_heads, key_heads, hots, delta_part = (
            attention_grads(
                query_block,
                keys_block,
                values_block,
                query_part,
                key_part,
                log_part,
                grad_part,
                table_cube,
                None,
            )
        )
        grad_query = jnp.einsum(
            "rhqk,rkhd->rqhd", grad_scores, key_heads, preferred_element_type=jnp.float32
        )
        grad_keys = jnp.einsum(
            "rhqk,rqhd->rkhd", grad_scores, query_heads, preferred_element_type=jnp.float32
        )
        grad_values = jnp.einsum(
            "rhqk,rqhd->rkhd",
            attention.astype(jnp.bfloat16),
            grad_heads,
            preferred_element_type=jnp.float32,
        )
        grad_table = table_sum(grad_scores, hots, table_cube)
        return (
            grad_query.reshape(query_block.shape),
            grad_keys.reshape(keys_block.shape),
            grad_values.reshape(keys_block.shape),
            grad_table,
        )

    grad_query_g, grad_keys_g, grad_values_g, grad_table_g = lax.map(
        backward_block,
        (
            grouped(queries),
            grouped(keys_all),
            grouped(values_all),
            side_groups,
            full_groups,
            log_total,
            grouped(grad_joined),
        ),
    )
    grad_table = jnp.sum(grad_table_g, axis=0)
    grad_keys_own, grad_values_own = (
        lax.psum_scatter(
            ungrouped(grad_keys_g).astype(jnp.bfloat16), "seq", scatter_dimension=1, tiled=True
        ).astype(jnp.float32),
        lax.psum_scatter(
            ungrouped(grad_values_g).astype(jnp.bfloat16), "seq", scatter_dimension=1, tiled=True
        ).astype(jnp.float32),
    )
    grad_query_scaled = (
        ungrouped(grad_query_g).astype(jnp.bfloat16).astype(jnp.float32) * query_scale
    )
    grad_keys_low = grad_keys_own.astype(jnp.bfloat16)
    grad_values_low = grad_values_own.astype(jnp.bfloat16)
    grad_b_query = jnp.sum(grad_query_scaled, axis=(0, 1))
    grad_b_value = jnp.sum(grad_values_low.astype(jnp.float32), axis=(0, 1))
    grad_joint = jnp.concatenate(
        [grad_query_scaled.astype(jnp.bfloat16), grad_keys_low, grad_values_low], axis=-1
    )
    grad_w_qkv = jnp.einsum(
        "rtd,rte->de", normed_low, grad_joint, preferred_element_type=jnp.float32
    )
    grad_normed = jnp.einsum("rte,de->rtd", grad_joint, w_qkv, preferred_element_type=jnp.float32)
    grad_inputs_in, grad_gain_one, grad_shift_one = norm_one_pull(grad_normed)
    tokens_grad = (grad_middle + grad_inputs_in).astype(jnp.bfloat16)
    shared = (
        lax.psum_scatter(grad_w_qkv, ("dp", "seq"), scatter_dimension=0, tiled=True),
        lax.psum_scatter(grad_b_query, ("dp", "seq"), scatter_dimension=0, tiled=True),
        lax.psum_scatter(grad_b_value, ("dp", "seq"), scatter_dimension=0, tiled=True),
        lax.psum_scatter(grad_w_proj, ("dp", "seq"), scatter_dimension=0, tiled=True),
        lax.psum_scatter(grad_b_proj, ("dp", "seq"), scatter_dimension=0, tiled=True),
        lax.psum_scatter(grad_w_up, ("dp", "seq"), scatter_dimension=0, tiled=True),
        lax.psum_scatter(grad_b_up, ("dp", "seq"), scatter_dimension=0, tiled=True),
        lax.psum_scatter(grad_w_down, ("dp", "seq"), scatter_dimension=0, tiled=True),
        lax.psum_scatter(grad_b_down, ("dp", "seq"), scatter_dimension=0, tiled=True),
        lax.psum_scatter(grad_gain_one, ("dp", "seq"), scatter_dimension=0, tiled=True),
        lax.psum_scatter(grad_shift_one, ("dp", "seq"), scatter_dimension=0, tiled=True),
        lax.psum_scatter(grad_gain_two, ("dp", "seq"), scatter_dimension=0, tiled=True),
        lax.psum_scatter(grad_shift_two, ("dp", "seq"), scatter_dimension=0, tiled=True),
        lax.psum_scatter(grad_layer_one, ("dp", "seq"), scatter_dimension=0, tiled=True),
        lax.psum_scatter(grad_layer_two, ("dp", "seq"), scatter_dimension=0, tiled=True),
    )
    table_total = lax.psum(grad_table, ("dp", "seq"))
    return (mixed, tokens_grad) + tuple(shared) + (table_total,)


def solution(mesh):
    in_specs = (
        P("dp", "seq", None),
        P("dp", None),
        P("dp", None),
        P(("dp", "seq"), None),
        P(("dp", "seq")),
        P(("dp", "seq")),
        P(("dp", "seq"), None),
        P(("dp", "seq")),
        P(("dp", "seq"), None),
        P(("dp", "seq")),
        P(("dp", "seq"), None),
        P(("dp", "seq")),
        P(("dp", "seq")),
        P(("dp", "seq")),
        P(("dp", "seq")),
        P(("dp", "seq")),
        P(("dp", "seq")),
        P(("dp", "seq")),
        P(),
        P("dp", "seq", None),
    )
    out_specs = (
        P("dp", "seq", None),
        P("dp", "seq", None),
        P(("dp", "seq"), None),
        P(("dp", "seq")),
        P(("dp", "seq")),
        P(("dp", "seq"), None),
        P(("dp", "seq")),
        P(("dp", "seq"), None),
        P(("dp", "seq")),
        P(("dp", "seq"), None),
        P(("dp", "seq")),
        P(("dp", "seq")),
        P(("dp", "seq")),
        P(("dp", "seq")),
        P(("dp", "seq")),
        P(("dp", "seq")),
        P(("dp", "seq")),
        P(),
    )
    return jax.shard_map(local, mesh=mesh, in_specs=in_specs, out_specs=out_specs, check_vma=False)
```

profile of v0, /device:TPU:0, one launch (start us, length us, event | category | flops | bytes accessed | tf_op | source)
XLA Modules:
  0.0 1275.2 jit_solution(2529064735616550257)
XLA Ops:
  17.2 42.8 %all-reduce.23 = (bf16[768]{0:T(1024)(128)(2,1)S(1)}, bf16[768]{0:T(1024)(128)(2,1)S(1)}, bf16[768]{0:T(1024)(128)(2,1)S(1)}, bf16[768]{0:T(1024)(128)(2,1)S(1)}...) all-reduce(bf16[768]{0:T(1024)(128)(2,1)S(1)} %dynamic-update-slice, ...), channel_id=1, replica_groups=mesh['dp'=8,'seq'=4] {'dp','seq'}, use_global_device_ids=true, to_apply=%add.2 | all-reduce | flops 10752 | bytes 43008
  63.2 10.7 all-gather.7.cloned.1.call-done
  84.0 16.8 %fusion = f32[2,144,576]{2,1,0:T(8,128)} fusion(s32[2,144,576]{2,1,0:T(8,128)S(1)} %get-tuple-element.174, bf16[47,47,12]{1,0,2:T(8,128)(2,1)S(1)} %reshape.289, s32[2,144,576]{2,0,1:T(2,128)S(1)} %copy.183), kind=kOutput, calls=%fused_computation.12 | convolution fusion | flops 779507712 | bytes 2150400 | tf_op jit(solution)/shard_map/while/body/eval_jaxpr/rqkb,ab->rqka/dot_general | solution.py:64
  100.8 16.8 %fusion.1 = f32[2,144,576]{2,1,0:T(8,128)} fusion(s32[2,144,576]{2,1,0:T(8,128)S(1)} %get-tuple-element.174, bf16[47,47,12]{1,0,2:T(8,128)(2,1)S(1)} %reshape.289, s32[2,144,576]{2,0,1:T(2,128)S(1)} %copy.183), kind=kOutput, calls=%fused_computation.13 | convolution fusion | flops 779507712 | bytes 2150400 | tf_op jit(solution)/shard_map/while/body/eval_jaxpr/rqkb,ab->rqka/dot_general | solution.py:64
  117.6 17.3 %fusion.2 = f32[2,144,576]{2,1,0:T(8,128)} fusion(s32[2,144,576]{2,1,0:T(8,128)S(1)} %get-tuple-element.174, bf16[47,47,12]{1,0,2:T(8,128)(2,1)S(1)} %reshape.289, s32[2,144,576]{2,0,1:T(2,128)S(1)} %copy.183), kind=kOutput, calls=%fused_computation.14 | convolution fusion | flops 779507712 | bytes 2150400 | tf_op jit(solution)/shard_map/while/body/eval_jaxpr/rqkb,ab->rqka/dot_general | solution.py:64
  134.9 16.8 %fusion.3 = f32[2,144,576]{2,1,0:T(8,128)} fusion(s32[2,144,576]{2,1,0:T(8,128)S(1)} %get-tuple-element.174, bf16[47,47,12]{1,0,2:T(8,128)(2,1)S(1)} %reshape.289, s32[2,144,576]{2,0,1:T(2,128)S(1)} %copy.183), kind=kOutput, calls=%fused_computation.15 | convolution fusion | flops 779507712 | bytes 2150400 | tf_op jit(solution)/shard_map/while/body/eval_jaxpr/rqkb,ab->rqka/dot_general | solution.py:64
  151.7 16.9 %fusion.4 = f32[2,144,576]{2,1,0:T(8,128)} fusion(s32[2,144,576]{2,1,0:T(8,128)S(1)} %get-tuple-element.174, bf16[47,47,12]{1,0,2:T(8,128)(2,1)S(1)} %reshape.289, s32[2,144,576]{2,0,1:T(2,128)S(1)} %copy.183), kind=kOutput, calls=%fused_computation.16 | convolution fusion | flops 779507712 | bytes 2150400 | tf_op jit(solution)/shard_map/while/body/eval_jaxpr/rqkb,ab->rqka/dot_general | solution.py:64
  168.6 16.8 %fusion.5 = f32[2,144,576]{2,1,0:T(8,128)} fusion(s32[2,144,576]{2,1,0:T(8,128)S(1)} %get-tuple-element.174, bf16[47,47,12]{1,0,2:T(8,128)(2,1)S(1)} %reshape.289, s32[2,144,576]{2,0,1:T(2,128)S(1)} %copy.183), kind=kOutput, calls=%fused_computation.17 | convolution fusion | flops 779507712 | bytes 2150400 | tf_op jit(solution)/shard_map/while/body/eval_jaxpr/rqkb,ab->rqka/dot_general | solution.py:64
  185.4 17.0 %fusion.6 = f32[2,144,576]{2,1,0:T(8,128)} fusion(s32[2,144,576]{2,1,0:T(8,128)S(1)} %get-tuple-element.174, bf16[47,47,12]{1,0,2:T(8,128)(2,1)S(1)} %reshape.289, s32[2,144,576]{2,0,1:T(2,128)S(1)} %copy.183), kind=kOutput, calls=%fused_computation.18 | convolution fusion | flops 779507712 | bytes 2150400 | tf_op jit(solution)/shard_map/while/body/eval_jaxpr/rqkb,ab->rqka/dot_general | solution.py:64
  202.4 16.8 %fusion.7 = f32[2,144,576]{2,1,0:T(8,128)} fusion(s32[2,144,576]{2,1,0:T(8,128)S(1)} %get-tuple-element.174, bf16[47,47,12]{1,0,2:T(8,128)(2,1)S(1)} %reshape.289, s32[2,144,576]{2,0,1:T(2,128)S(1)} %copy.183), kind=kOutput, calls=%fused_computation.19 | convolution fusion | flops 779507712 | bytes 2150400 | tf_op jit(solution)/shard_map/while/body/eval_jaxpr/rqkb,ab->rqka/dot_general | solution.py:64
  219.2 17.2 %fusion.8 = f32[2,144,576]{2,1,0:T(8,128)} fusion(s32[2,144,576]{2,1,0:T(8,128)S(1)} %get-tuple-element.174, bf16[47,47,12]{1,0,2:T(8,128)(2,1)S(1)} %reshape.289, s32[2,144,576]{2,0,1:T(2,128)S(1)} %copy.183), kind=kOutput, calls=%fused_computation.20 | convolution fusion | flops 779507712 | bytes 2150400 | tf_op jit(solution)/shard_map/while/body/eval_jaxpr/rqkb,ab->rqka/dot_general | solution.py:64
  236.4 15.9 %fusion.9 = f32[2,144,576]{2,1,0:T(8,128)S(1)} fusion(s32[2,144,576]{2,1,0:T(8,128)S(1)} %get-tuple-element.174, bf16[47,47,12]{1,0,2:T(8,128)(2,1)S(1)} %reshape.289, s32[2,144,576]{2,0,1:T(2,128)S(1)} %copy.183), kind=kOutput, calls=%fused_computation.21 | convolution fusion | flops 779507712 | bytes 2150400 | tf_op jit(solution)/shard_map/while/body/eval_jaxpr/rqkb,ab->rqka/dot_general | solution.py:64
  252.3 16.1 %fusion.10 = f32[2,144,576]{2,1,0:T(8,128)S(1)} fusion(s32[2,144,576]{2,1,0:T(8,128)S(1)} %get-tuple-element.174, bf16[47,47,12]{1,0,2:T(8,128)(2,1)S(1)} %reshape.289, s32[2,144,576]{2,0,1:T(2,128)S(1)} %copy.183), kind=kOutput, calls=%fused_computation.22 | convolution fusion | flops 779507712 | bytes 2150400 | tf_op jit(solution)/shard_map/while/body/eval_jaxpr/rqkb,ab->rqka/dot_general | solution.py:64
  268.5 16.1 %fusion.11 = f32[2,144,576]{2,1,0:T(8,128)S(1)} fusion(s32[2,144,576]{2,1,0:T(8,128)S(1)} %get-tuple-element.174, bf16[47,47,12]{1,0,2:T(8,128)(2,1)S(1)} %reshape.289, s32[2,144,576]{2,0,1:T(2,128)S(1)} %copy.183), kind=kOutput, calls=%fused_computation.23 | convolution fusion | flops 779507712 | bytes 2150400 | tf_op jit(solution)/shard_map/while/body/eval_jaxpr/rqkb,ab->rqka/dot_general | solution.py:64
  490.9 10.1 fusion.128
  502.1 9.8 fusion.131
  512.9 9.8 fusion.134
  523.8 9.8 fusion.137
  534.6 9.8 fusion.140
  544.8 9.9 fusion.143
  555.1 9.8 fusion.146
  565.3 9.8 fusion.149
  575.6 9.8 fusion.152
  585.8 9.8 fusion.155
  596.2 10.0 fusion.158
  606.7 9.9 fusion.161
  659.1 40.1 %all-reduce.22 = (f32[768]{0:T(1024)S(1)}, f32[768]{0:T(1024)S(1)}, f32[768]{0:T(1024)S(1)}, f32[3072]{0:T(1024)S(1)}, f32[768]{0:T(1024)S(1)}, /*index=5*/f32[7...) all-reduce(f32[768]{0:T(1024)S(1)} %reduce_sum.474, ...), channel_id=5, replica_groups=mesh['dp'=8,'seq'=4] {'dp','seq'}, use_global_device_ids=true, to_apply=%region_32.33.clone | all-reduce | flops 10752 | bytes 86016
  705.6 46.2 %all-reduce.26.cloned.1.call-done = f32[2209,12]{0,1:T(8,128)} async-done(((f32[2209,12]{0,1:T(8,128)}), f32[2209,12]{0,1:T(8,128)}) %all-reduce.26.cloned.1.call-update) | async-done | bytes 106048 | tf_op jit(solution)/shard_map/psum | solution.py:398
  751.8 106.8 %reduce-scatter.13.cloned.1.call-done = f32[24,768]{1,0:T(8,128)} async-done(((f32[768,768]{1,0:T(8,128)}), f32[24,768]{1,0:T(8,128)}) %reduce-scatter.13.cloned.1.call-update) | async-done | bytes 73744 | tf_op jit(solution)/shard_map/reduce_scatter | solution.py:385
  858.6 142.0 %reduce-scatter.15.cloned.1.call-done = f32[24,3072]{1,0:T(8,128)} async-done(((f32[768,3072]{1,0:T(8,128)}), f32[24,3072]{1,0:T(8,128)}) %reduce-scatter.15.cloned.1.call-update) | async-done | bytes 294928 | tf_op jit(solution)/shard_map/reduce_scatter | solution.py:387
  1000.6 141.0 %reduce-scatter.17.cloned.1.call-done = f32[96,768]{1,0:T(8,128)} async-done(((f32[3072,768]{1,0:T(8,128)}), f32[96,768]{1,0:T(8,128)}) %reduce-scatter.17.cloned.1.call-update) | async-done | bytes 294928 | tf_op jit(solution)/shard_map/reduce_scatter | solution.py:389
  1141.6 125.2 %reduce-scatter.11.cloned.1.call-done = f32[24,2304]{1,0:T(8,128)} async-done(((f32[768,2304]{1,0:T(8,128)}), f32[24,2304]{1,0:T(8,128)}) %reduce-scatter.11.cloned.1.call-update) | async-done | bytes 221200 | tf_op jit(solution)/shard_map/reduce_scatter | solution.py:382
  (361 shorter events, 285.9 us)
Async XLA Ops:
  7.2 74.2 %copy-start.67 = (s32[2,4]{1,0:T(2,128)S(1)}, s32[2,4]{1,0:T(2,128)}, u32[]{:S(2)}) copy-start(s32[2,4]{1,0:T(2,128)} %param.21) | copy-start | bytes 100
  7.2 74.5 %copy-start.40 = (bf16[2209,12]{0,1:T(8,128)(2,1)S(1)}, bf16[2209,12]{0,1:T(8,128)(2,1)}, u32[]{:S(2)}) copy-start(bf16[2209,12]{0,1:T(8,128)(2,1)} %param.38) | copy-start | bytes 159052
  7.2 74.8 %copy-start.82 = (s32[2,4]{1,0:T(2,128)S(1)}, s32[2,4]{1,0:T(2,128)}, u32[]{:S(2)}) copy-start(s32[2,4]{1,0:T(2,128)} %param.22) | copy-start | bytes 100
  7.2 66.7 %all-gather.7.cloned.1.call-start = ((), (), s32[]{:S(2)}) async-start(), calls=%async_computation.6 | async-start | bytes 3649536 | tf_op jit(solution)/shard_map/all_gather | solution.py:148
  8.0 398.1 %all-gather.9.cloned.1.call-start = ((), (), s32[]{:S(2)}) async-start(), calls=%async_computation.7 | async-start | bytes 2211840 | tf_op jit(solution)/shard_map/all_gather | solution.py:212
  60.1 40.7 %copy-start.68 = (f32[768]{0:T(1024)}, f32[768]{0:T(1024)S(1)}, u32[]{:S(2)}) copy-start(f32[768]{0:T(1024)S(1)} %convert_element_type.196) | copy-start | bytes 9220
  60.1 40.7 %copy-start.53 = (f32[768]{0:T(1024)}, f32[768]{0:T(1024)S(1)}, u32[]{:S(2)}) copy-start(f32[768]{0:T(1024)S(1)} %convert_element_type.195) | copy-start | bytes 9220
  61.3 39.5 %copy-start.47 = (f32[2,144]{1,0:T(2,128)}, f32[2,144]{1,0:T(2,128)S(1)}, u32[]{:S(2)}) copy-start(f32[2,144]{1,0:T(2,128)S(1)} %broadcast_multiply_fusion.1) | copy-start | bytes 3460
  63.2 37.6 %copy-start.60 = (f32[2,144]{1,0:T(2,128)}, f32[2,144]{1,0:T(2,128)S(1)}, u32[]{:S(2)}) copy-start(f32[2,144]{1,0:T(2,128)S(1)} %fusion.188) | copy-start | bytes 3460
  78.4 331.5 %all-gather.11.cloned.1.call-start = ((), (), s32[]{:S(2)}) async-start(), calls=%async_computation.8 | async-start | bytes 2211840 | tf_op jit(solution)/shard_map/all_gather | solution.py:211
  79.3 346.6 %all-gather.13.cloned.1.call-start = ((), (), s32[]{:S(2)}) async-start(), calls=%async_computation.9 | async-start | bytes 1216512 | tf_op jit(solution)/shard_map/all_gather | solution.py:151
  79.9 350.8 %all-gather.15.cloned.1.call-start = ((), (), s32[]{:S(2)}) async-start(), calls=%async_computation.10 | async-start | bytes 4866048 | tf_op jit(solution)/shard_map/all_gather | solution.py:153
  80.5 366.3 %all-gather.17.cloned.1.call-start = ((), (), s32[]{:S(2)}) async-start(), calls=%async_computation.11 | async-start | bytes 4866048 | tf_op jit(solution)/shard_map/all_gather | solution.py:155
  81.1 561.2 %reduce-scatter.9.cloned.1.call-start = ((), (), s32[]{:S(2)}) async-start(), calls=%async_computation.13 | async-start | bytes 2211840 | tf_op jit(solution)/shard_map/reduce_scatter | solution.py:361
  84.0 184.4 %copy-start.28 = (s32[2,144,576]{2,0,1:T(2,128)}, s32[2,144,576]{2,0,1:T(2,128)S(1)}, u32[]{:S(2)}) copy-start(s32[2,144,576]{2,0,1:T(2,128)S(1)} %copy.183) | copy-start | bytes 1990660
  377.7 17.2 %copy-start.81 = (bf16[768]{0:T(1024)(128)(2,1)S(1)}, bf16[768]{0:T(1024)(128)(2,1)}, u32[]{:S(2)}) copy-start(bf16[768]{0:T(1024)(128)(2,1)} %get-tuple-element.139) | copy-start | bytes 4612
  377.7 17.2 %copy-start.80 = (bf16[768]{0:T(1024)(128)(2,1)S(1)}, bf16[768]{0:T(1024)(128)(2,1)}, u32[]{:S(2)}) copy-start(bf16[768]{0:T(1024)(128)(2,1)} %get-tuple-element.138) | copy-start | bytes 4612
  377.7 17.2 %copy-start.79 = (bf16[768]{0:T(1024)(128)(2,1)S(1)}, bf16[768]{0:T(1024)(128)(2,1)}, u32[]{:S(2)}) copy-start(bf16[768]{0:T(1024)(128)(2,1)} %get-tuple-element.142) | copy-start | bytes 4612
  377.7 17.2 %copy-start.66 = (bf16[3072]{0:T(1024)(128)(2,1)S(1)}, bf16[3072]{0:T(1024)(128)(2,1)}, u32[]{:S(2)}) copy-start(bf16[3072]{0:T(1024)(128)(2,1)} %get-tuple-element.140) | copy-start | bytes 18436
  377.7 17.8 %copy-start.78 = (bf16[768]{0:T(1024)(128)(2,1)S(1)}, bf16[768]{0:T(1024)(128)(2,1)}, u32[]{:S(2)}) copy-start(bf16[768]{0:T(1024)(128)(2,1)} %get-tuple-element.141) | copy-start | bytes 4612
  377.8 18.4 %copy-start.77 = (bf16[768]{0:T(1024)(128)(2,1)S(1)}, bf16[768]{0:T(1024)(128)(2,1)}, u32[]{:S(2)}) copy-start(bf16[768]{0:T(1024)(128)(2,1)} %get-tuple-element.144) | copy-start | bytes 4612
  394.9 64.7 %copy-start.55 = (f32[768]{0:T(1024)}, f32[768]{0:T(1024)S(1)}, u32[]{:S(2)}) copy-start(f32[768]{0:T(1024)S(1)} %convert_element_type.212) | copy-start | bytes 9220
  396.2 50.6 %copy-start.70 = (f32[768]{0:T(1024)}, f32[768]{0:T(1024)S(1)}, u32[]{:S(2)}) copy-start(f32[768]{0:T(1024)S(1)} %convert_element_type.211) | copy-start | bytes 9220
  429.0 30.6 %copy-start.4 = (f32[2,144,768]{2,1,0:T(8,128)}, f32[2,144,768]{2,1,0:T(8,128)S(1)}, u32[]{:S(2)}) copy-start(f32[2,144,768]{2,1,0:T(8,128)S(1)} %get-tuple-element.152) | copy-start | bytes 2654212
  429.0 30.6 %copy-start.51 = (f32[2,144]{1,0:T(2,128)}, f32[2,144]{1,0:T(2,128)S(1)}, u32[]{:S(2)}) copy-start(f32[2,144]{1,0:T(2,128)S(1)} %broadcast_multiply_fusion) | copy-start | bytes 3460
  429.3 30.4 %copy-start.64 = (f32[2,144]{1,0:T(2,128)}, f32[2,144]{1,0:T(2,128)S(1)}, u32[]{:S(2)}) copy-start(f32[2,144]{1,0:T(2,128)S(1)} %fusion.189) | copy-start | bytes 3460
  485.2 157.2 %reduce-scatter.7.cloned.1.call-start = ((), (), s32[]{:S(2)}) async-start(), calls=%async_computation.12 | async-start | bytes 2211840 | tf_op jit(solution)/shard_map/reduce_scatter | solution.py:358
  596.1 155.7 %all-reduce.26.cloned.1.call-start = ((), (), s32[]{:S(2)}) async-start(), calls=%async_computation.18 | async-start | bytes 294912 | tf_op jit(solution)/shard_map/psum | solution.py:398
  618.2 240.4 %reduce-scatter.13.cloned.1.call-start = ((), (), s32[]{:S(2)}) async-start(), calls=%async_computation.15 | async-start | bytes 2433024 | tf_op jit(solution)/shard_map/reduce_scatter | solution.py:385
  620.6 380.1 %reduce-scatter.15.cloned.1.call-start = ((), (), s32[]{:S(2)}) async-start(), calls=%async_computation.16 | async-start | bytes 9732096 | tf_op jit(solution)/shard_map/reduce_scatter | solution.py:387
  627.5 514.2 %reduce-scatter.17.cloned.1.call-start = ((), (), s32[]{:S(2)}) async-start(), calls=%async_computation.17 | async-start | bytes 9732096 | tf_op jit(solution)/shard_map/reduce_scatter | solution.py:389
  635.5 631.3 %reduce-scatter.11.cloned.1.call-start = ((), (), s32[]{:S(2)}) async-start(), calls=%async_computation.14 | async-start | bytes 7299072 | tf_op jit(solution)/shard_map/reduce_scatter | solution.py:382
  (68 other events, 551.1 us)
Sparse Core Ops, SparseCore 0:
  11.0 62.9 all-gather.6
  78.5 19.7 all-gather.8
  99.9 20.7 all-gather.10
  123.4 54.0 all-gather.12
  180.2 62.5 all-gather.14
  245.6 62.4 all-gather.16
  485.3 28.4 reduce-scatter.8
  596.2 28.5 reduce-scatter.6
  631.0 120.7 all-reduce.25
  757.5 101.0 reduce-scatter.12
  866.1 134.5 reduce-scatter.14
  1007.0 134.6 reduce-scatter.16
  1148.8 117.9 reduce-scatter.10
where the time goes:
time: 1280 us
  waiting for transfers between devices  574 us (45%)
  matrix products  406 us (32%)
  other arithmetic  125 us (10%)
  blocking collectives  82.9 us (6%)
  local copies, waits for them, and re-layouts  70.2 us (5%)
  between operations  15.6 us (1%)
    dot_general x12, matrix products, bias_offsets(): jnp.einsum('rqkb,ab->rqka', cols_hot, table_cube[:, :, head], preferred_e...  201 us
    reduce_scatter x1, waiting for transfers between devices, local(): lax.psum_scatter(grad_w_up, ('dp', 'seq'), scatter_dimension=0, tiled=True)  142 us
    reduce_scatter x1, waiting for transfers between devices, local(): lax.psum_scatter(grad_w_down, ('dp', 'seq'), scatter_dimension=0, tiled=T...  141 us
    reduce_scatter x1, waiting for transfers between devices, local(): lax.psum_scatter(grad_w_qkv, ('dp', 'seq'), scatter_dimension=0, tiled=True)  125 us
    dot_general x12, matrix products, table_sum(): jnp.einsum('rqka,rqkb->ab', rows_hot, weighted, preferred_element_type=jn...  118 us
    reduce_scatter x1, waiting for transfers between devices, local(): lax.psum_scatter(grad_w_proj, ('dp', 'seq'), scatter_dimension=0, tiled=T...  107 us
    dot_general x12, other arithmetic, table_sum(): jnp.einsum('rqka,rqkb->ab', rows_hot, weighted, preferred_element_type=jn...  102 us
    unnamed x2, blocking collectives  82.9 us
  transfers between devices with their start and end apart: 13, of which 6 were waited for; matrix products, arithmetic and copies ran while one was open for 43% of the time, Pallas kernels for 0%

commit v1 on v0

v1 whole, which is shorter than its diff:
```python
import functools

import jax
import jax.numpy as jnp
from jax import lax
from jax.experimental import pallas as pl
from jax.experimental.pallas import tpu as pltpu
from jax.sharding import PartitionSpec as P

GRID = 24
SIDE = 2 * GRID - 1
ROW_LEN = 576
IMGS = 4
EPS = 1e-06
STRIP = 640
BLOCKS = 11
BF = jnp.bfloat16
F32 = jnp.float32
BOTH = ("dp", "seq")


def norm_rows(values, gain_vec, offset_vec):
    center = values - jnp.mean(values, axis=-1, keepdims=True)
    spread = jnp.mean(center * center, axis=-1, keepdims=True)
    return center * lax.rsqrt(spread + EPS) * gain_vec + offset_vec


def layout(lengths, widths):
    ends = jnp.cumsum(lengths).astype(jnp.int32)
    starts = ends - lengths
    total = ends[-1]
    full = jnp.full((1,), ROW_LEN, jnp.int32)
    meta = jnp.stack(
        [
            jnp.concatenate([starts, total[None]]),
            jnp.concatenate([ends, full]),
            jnp.concatenate([starts, jnp.zeros((1,), jnp.int32)]),
            jnp.concatenate([widths, jnp.full((1,), GRID, jnp.int32)]),
        ]
    ).astype(jnp.int32)
    places = jnp.arange(ROW_LEN, dtype=jnp.int32)
    segment = jnp.sum((places[:, None] >= ends[None, :]).astype(jnp.int32), axis=1)
    return meta, segment


def strip_range(b, e):
    length = e - b
    return (STRIP - length) // 128, jnp.minimum((STRIP + length + GRID) // 128, BLOCKS - 1)


def strip_onehot(block, w, depth):
    lane = lax.broadcasted_iota(jnp.int32, (1, 128), 1) + (block * 128 - STRIP + 80 * w)
    line = jnp.floor((lane.astype(F32) + 0.5) / jnp.full((1, 128), w, jnp.int32).astype(F32)).astype(jnp.int32)
    column = lane - line * w
    level = jnp.clip(80 - line, 1 - GRID, GRID - 1) + (GRID - 1)
    code = level * GRID + column
    return (lax.broadcasted_iota(jnp.int32, (depth, 128), 0) == code).astype(F32).astype(BF)


def attn_fwd_kernel(meta, tab, q, k, v, seg_col, seg_row, p_out, o_out, strip, bias):
    heads = p_out.shape[0]
    depth = tab.shape[1]
    lane = lax.broadcasted_iota(jnp.int32, (1, 128), 1)
    for g in range(IMGS + 1):
        b, e, s, w = meta[0, g], meta[1, g], meta[2, g], meta[3, g]
        low, high = strip_range(b, e)

        def build(block, carry, w=w):
            strip[block] = jnp.dot(tab[...], strip_onehot(block, w, depth), preferred_element_type=F32)
            return carry

        lax.fori_loop(low, jnp.where(e > b, high + 1, low), build, 0)

        def line(y, carry, b=b, e=e, s=s, w=w, g=g):
            p0 = s + y * w
            off = STRIP - p0
            j0 = off // 128
            r = off - j0 * 128
            shift = (128 - r) % 128

            def part(kb, inner):
                mixed = jnp.where(lane >= r, strip[j0 + kb], strip[j0 + kb + 1])
                moved = pltpu.roll(mixed, shift, 1)
                for h in range(heads):
                    piece = moved[h * GRID : (h + 1) * GRID]
                    if g == IMGS:
                        piece = jnp.where(lane + kb * 128 >= b, piece, bias[h, kb, pl.ds(p0, GRID), :])
                    bias[h, kb, pl.ds(p0, GRID), :] = piece
                return inner

            lax.fori_loop(b // 128, (e - 1) // 128 + 1, part, 0)
            return carry

        lax.fori_loop((b - s) // w, jnp.where(e > b, (e - 1 - s) // w + 1, 0), line, 0)

    rows = 144
    half = lax.broadcasted_iota(jnp.int32, (1, 128), 1) < 64
    for t in range(heads // 2):
        cols = slice(128 * t, 128 * t + 128)

        def chunk(i, carry, t=t, cols=cols):
            r0 = pl.multiple_of(i * rows, 16)
            here = pl.ds(r0, rows)
            q_tile = q[here, cols]
            outs = []
            for sub in range(2):
                h = 2 * t + sub
                q_own = jnp.where(half if sub == 0 else ~half, q_tile, jnp.zeros_like(q_tile))
                score = lax.dot_general(q_own, k[:, cols], (((1,), (1,)), ((), ())), preferred_element_type=F32)
                offs = jnp.concatenate([bias[h, kb, here, :] for kb in range(5)], axis=1)[:, :ROW_LEN]
                score = jnp.where(seg_col[here, :] == seg_row[...], score + offs, -1e30)
                top = jnp.max(score, axis=1, keepdims=True)
                raised = jnp.exp(score - top)
                prob = (raised / jnp.sum(raised, axis=1, keepdims=True)).astype(BF)
                p_out[h, here, :] = prob
                outs.append(jnp.dot(prob, v[:, cols], preferred_element_type=F32))
            o_out[here, cols] = jnp.where(half, outs[0], outs[1]).astype(BF)
            return carry

        lax.fori_loop(0, ROW_LEN // rows, chunk, 0)


def attn_bwd_kernel(meta, q, k, v, do, p, dq_out, dk_out, dv_out, grid_out, strip, dscore, ds_low, dkt, dvt):
    heads = p.shape[0]
    depth = grid_out.shape[1]
    rows = 144
    lane = lax.broadcasted_iota(jnp.int32, (1, 128), 1)
    half = lane < 64
    for t in range(heads // 2):
        cols = slice(128 * t, 128 * t + 128)
        q_turn = jnp.transpose(q[:, cols].astype(F32)).astype(BF)
        do_turn = jnp.transpose(do[:, cols].astype(F32)).astype(BF)
        for sub in range(2):
            h = 2 * t + sub

            def chunk(i, carry, h=h, sub=sub, cols=cols):
                here = pl.ds(pl.multiple_of(i * rows, 16), rows)
                do_tile = do[here, cols]
                do_own = jnp.where(half if sub == 0 else ~half, do_tile, jnp.zeros_like(do_tile))
                d_prob = lax.dot_general(do_own, v[:, cols], (((1,), (1,)), ((), ())), preferred_element_type=F32)
                prob = p[h, here, :].astype(F32)
                weighted = prob * d_prob
                delta = jnp.sum(weighted, axis=1, keepdims=True)
                low = (weighted - prob * delta).astype(BF)
                ds_low[sub, here, :] = low
                wide = low.astype(F32)
                for kb in range(4):
                    dscore[h, kb, here, :] = wide[:, 128 * kb : 128 * kb + 128]
                dscore[h, 4, here, 0:64] = wide[:, 512:576]
                return carry

            lax.fori_loop(0, ROW_LEN // rows, chunk, 0)
            feats = slice(64 * sub, 64 * sub + 64)
            own = slice(64 * h, 64 * h + 64)
            dkt[own, :] = jnp.dot(q_turn[feats], ds_low[sub], preferred_element_type=F32)
            dvt[own, :] = jnp.dot(do_turn[feats], p[h], preferred_element_type=F32)

        def query(i, carry, cols=cols):
            here = pl.ds(pl.multiple_of(i * rows, 16), rows)
            even = jnp.dot(ds_low[0, here, :], k[:, cols], preferred_element_type=F32)
            odd = jnp.dot(ds_low[1, here, :], k[:, cols], preferred_element_type=F32)
            dq_out[here, cols] = jnp.where(half, even, odd).astype(BF)
            return carry

        lax.fori_loop(0, ROW_LEN // rows, query, 0)
        dk_out[:, cols] = jnp.transpose(dkt[128 * t : 128 * t + 128, :]).astype(BF)
        dv_out[:, cols] = jnp.transpose(dvt[128 * t : 128 * t + 128, :]).astype(BF)

    grid_out[...] = jnp.zeros_like(grid_out)
    dscore[:, :, ROW_LEN:, :] = jnp.zeros(dscore.shape[:2] + (dscore.shape[2] - ROW_LEN, 128), F32)
    column = lax.broadcasted_iota(jnp.int32, (GRID, 128), 0)
    for g in range(IMGS + 1):
        b, e, s, w = meta[0, g], meta[1, g], meta[2, g], meta[3, g]
        low, high = strip_range(b, e)
        stop = jnp.where(e > b, high + 1, low)

        def clear(block, carry):
            strip[block] = jnp.zeros(strip.shape[1:], F32)
            return carry

        lax.fori_loop(low, stop, clear, 0)

        def line(y, carry, b=b, e=e, s=s, w=w):
            p0 = s + y * w
            off = STRIP - p0
            j0 = off // 128
            r = off - j0 * 128

            def part(kb, inner):
                place = lane + kb * 128
                keep = (column < w) & (place >= b) & (place < e)
                for h in range(heads):
                    rows_h = slice(h * GRID, (h + 1) * GRID)
                    piece = jnp.where(keep, dscore[h, kb, pl.ds(p0, GRID), :], 0.0)
                    moved = pltpu.roll(piece, r, 1)
                    strip[j0 + kb, rows_h, :] += jnp.where(lane >= r, moved, 0.0)
                    strip[j0 + kb + 1, rows_h, :] += jnp.where(lane >= r, 0.0, moved)
                return inner

            lax.fori_loop(b // 128, (e - 1) // 128 + 1, part, 0)
            return carry

        lax.fori_loop((b - s) // w, jnp.where(e > b, (e - 1 - s) // w + 1, 0), line, 0)

        def fold(block, carry, w=w):
            grid_out[...] += lax.dot_general(
                strip[block].astype(BF),
                strip_onehot(block, w, depth),
                (((1,), (1,)), ((), ())),
                preferred_element_type=F32,
            )
            return carry

        lax.fori_loop(low, stop, fold, 0)


def vmem():
    return pl.BlockSpec(memory_space=pltpu.VMEM)


def attn_fwd(meta, tab, q, k, v, segment):
    heads = tab.shape[0] // GRID
    return pl.pallas_call(
        attn_fwd_kernel,
        out_shape=(
            jax.ShapeDtypeStruct((heads, ROW_LEN, ROW_LEN), BF),
            jax.ShapeDtypeStruct(q.shape, BF),
        ),
        in_specs=[pl.BlockSpec(memory_space=pltpu.SMEM)] + [vmem()] * 6,
        out_specs=(vmem(), vmem()),
        scratch_shapes=[
            pltpu.VMEM((BLOCKS, heads * GRID, 128), F32),
            pltpu.VMEM((heads, 5, ROW_LEN + 32, 128), F32),
        ],
        compiler_params=pltpu.CompilerParams(vmem_limit_bytes=48 * 1024 * 1024),
        cost_estimate=pl.CostEstimate(flops=2_000_000_000, bytes_accessed=8_000_000, transcendentals=2_000_000),
        name="attn_fwd",
    )(meta, tab, q, k, v, segment[:, None], segment[None, :])


def attn_bwd(meta, q, k, v, do, p, depth):
    heads = p.shape[0]
    low = jax.ShapeDtypeStruct(q.shape, BF)
    return pl.pallas_call(
        attn_bwd_kernel,
        out_shape=(low, low, low, jax.ShapeDtypeStruct((heads * GRID, depth), F32)),
        in_specs=[pl.BlockSpec(memory_space=pltpu.SMEM)] + [vmem()] * 5,
        out_specs=(vmem(),) * 4,
        scratch_shapes=[
            pltpu.VMEM((BLOCKS, heads * GRID, 128), F32),
            pltpu.VMEM((heads, 5, ROW_LEN + 32, 128), F32),
            pltpu.VMEM((2, ROW_LEN, ROW_LEN), BF),
            pltpu.VMEM((heads * 64, ROW_LEN), F32),
            pltpu.VMEM((heads * 64, ROW_LEN), F32),
        ],
        compiler_params=pltpu.CompilerParams(vmem_limit_bytes=48 * 1024 * 1024),
        cost_estimate=pl.CostEstimate(flops=5_000_000_000, bytes_accessed=8_000_000, transcendentals=0),
        name="attn_bwd",
    )(meta, q, k, v, do, p)


def reorder_kernel(to_out, places, src, dst):
    for i in range(16):
        j = places[i]
        if to_out:
            dst[j] = src[i]
        else:
            dst[i] = src[j]


def reorder(blocks, places, to_out):
    size = blocks.size * 2
    return pl.pallas_call(
        functools.partial(reorder_kernel, to_out),
        out_shape=jax.ShapeDtypeStruct(blocks.shape, blocks.dtype),
        in_specs=[pl.BlockSpec(memory_space=pltpu.SMEM), vmem()],
        out_specs=vmem(),
        compiler_params=pltpu.CompilerParams(vmem_limit_bytes=16 * 1024 * 1024),
        cost_estimate=pl.CostEstimate(flops=0, bytes_accessed=2 * size, transcendentals=0),
        name="reorder",
    )(places, blocks)


class Net:
    def __init__(self, dp, seq):
        self.dp, self.seq = dp, seq
        self.fast = dp == 8
        at_seq = lax.axis_index("seq")
        self.core = at_seq % 2
        self.x = at_seq // 2
        at_dp = lax.axis_index("dp")

        def table(fn):
            pairs = []
            for d in range(dp):
                for s in range(seq):
                    d2, s2 = fn(d, s)
                    pairs.append((d * seq + s, d2 * seq + s2))
            return pairs

        self.to_core = table(lambda d, s: (d, s ^ 1))
        self.to_x = table(lambda d, s: (d, s ^ 2))
        if self.fast:
            self.phases = (
                table(lambda d, s: (d ^ 4, s)),
                table(lambda d, s: (d ^ 2, s)),
                table(lambda d, s: (d, s ^ 2) if s % 2 == 0 else (d ^ 1, s)),
                table(lambda d, s: (d ^ 1, s) if s % 2 == 0 else (d, s ^ 2)),
            )
            rel = jnp.arange(16, dtype=jnp.int32)
            d1, d2, d3, d4 = rel % 2, (rel // 2) % 2, (rel // 4) % 2, rel // 8
            by_x = jnp.where(self.core == 0, d3, d4)
            by_y = jnp.where(self.core == 0, d4, d3)
            self.places = ((at_dp * 2 + self.x) ^ (d1 * 8 + d2 * 4 + by_y * 2 + by_x)).astype(jnp.int32)

    def send(self, array, pairs):
        return lax.ppermute(array, BOTH, pairs)

    def by_core(self, own, other, axis):
        first = self.core == 0
        return jnp.stack([jnp.where(first, own, other), jnp.where(first, other, own)], axis=axis)

    def pick(self, array, index, axis):
        return lax.dynamic_index_in_dim(array, index, axis, keepdims=False)

    def gather(self, block):
        if self.fast:
            for pairs in self.phases:
                block = jnp.stack([block, self.send(block, pairs)])
            shape = block.shape[4:]
            return reorder(block.reshape((16,) + shape), self.places, True).reshape((self.dp, 2) + shape)
        block = lax.all_gather(block, "dp", axis=0)
        other = self.send(block, self.to_x)
        first = self.x == 0
        return jnp.stack([jnp.where(first, block, other), jnp.where(first, other, block)], axis=1)

    def reduce(self, blocks):
        shape = blocks.shape[2:]
        if self.fast:
            blocks = reorder(blocks.reshape((16,) + shape), self.places, False)
            for step in (3, 2, 1, 0):
                blocks = blocks.reshape((2, 2**step) + shape)
                came = self.send(blocks[1], self.phases[step])
                blocks = blocks[0].astype(F32) + came.astype(F32)
                if step:
                    blocks = blocks.astype(BF)
            return blocks.reshape(shape)
        came = self.send(self.pick(blocks, 1 - self.x, 1), self.to_x)
        summed = self.pick(blocks, self.x, 1).astype(F32) + came.astype(F32)
        return lax.psum_scatter(summed, "dp", scatter_dimension=0, tiled=False)

    def total(self, array):
        if self.fast:
            for pairs in self.phases:
                array = array + self.send(array, pairs)
            return array
        array = array + self.send(array, self.to_x)
        return lax.psum(array, "dp")


def wide(array):
    return array.astype(F32)


def dot(a, b):
    return jnp.dot(a, b, preferred_element_type=F32)


def dot_t(a, b):
    return lax.dot_general(a, b, (((0,), (0,)), ((), ())), preferred_element_type=F32)


def dot_r(a, b):
    return lax.dot_general(a, b, (((1,), (1,)), ((), ())), preferred_element_type=F32)


def local(
    dp,
    seq,
    tokens,
    image_lengths,
    grid_widths,
    qkv_weight,
    q_bias,
    v_bias,
    proj_weight,
    proj_bias,
    fc1_weight,
    fc1_bias,
    fc2_weight,
    fc2_bias,
    norm1_gain,
    norm1_bias,
    norm2_gain,
    norm2_bias,
    scale1,
    scale2,
    bias_table,
    out_grad,
):
    net = Net(dp, seq)
    core, at_x = net.core, net.x
    row_count, shard, width = tokens.shape
    heads = bias_table.shape[1]
    own_heads = heads // 2
    own_feats = width // 2
    scale = (width // heads) ** (-0.5)
    n_dev = dp * seq
    rows_w = width // n_dev
    ff = fc2_weight.shape[0] * n_dev
    rows_f = ff // n_dev
    chips = n_dev // 2

    small = [q_bias, v_bias, proj_bias, fc2_bias, norm1_gain, norm1_bias, norm2_gain, norm2_bias, scale1, scale2, fc1_bias]
    small = jnp.concatenate(small)
    n_small = small.shape[0]
    pack_rows = -(-(rows_w + 1) // 16) * 16
    pack = jnp.concatenate(
        [proj_weight, jnp.pad(small, (0, width - n_small))[None], jnp.zeros((pack_rows - rows_w - 1, width), BF)]
    )
    qkv_view = qkv_weight.reshape(rows_w, 3, 2, own_feats)
    qkv_block = net.by_core(
        net.pick(qkv_view, core, 2), net.send(net.pick(qkv_view, 1 - core, 2), net.to_core), 0
    ).reshape(2 * rows_w, 3 * own_feats)
    fc1_view = fc1_weight.reshape(rows_w, chips, 2, rows_f)
    fc1_block = net.by_core(
        net.pick(fc1_view, core, 2), net.send(net.pick(fc1_view, 1 - core, 2), net.to_core), 0
    ).reshape(2 * rows_w, ff // 2)

    pack_all = net.gather(pack)
    w_qkv = net.gather(qkv_block).reshape(width, 3 * own_feats)
    pack_all = net.by_core(pack_all, net.send(pack_all, net.to_core), 2)
    w_proj = pack_all[:, :, :, :rows_w].reshape(width, width)
    vectors = pack_all[:, :, :, rows_w, :n_small]
    whole = [vectors[..., j * rows_w : (j + 1) * rows_w].reshape(width) for j in range(10)]
    b_query, b_value, b_proj, b_down, gain_one, shift_one, gain_two, shift_two, layer_one, layer_two = [wide(a) for a in whole]
    b_up = wide(net.pick(vectors[..., 10 * rows_w :], core, 2).reshape(ff // 2))
    b_query = lax.dynamic_slice_in_dim(b_query, core * own_feats, own_feats)
    b_value = lax.dynamic_slice_in_dim(b_value, core * own_feats, own_feats)
    w_up = net.gather(fc1_block).reshape(width, ff // 2)
    w_down = net.gather(fc2_weight).reshape(ff // 2, width)

    def to_own(array):
        mine, theirs = net.pick(array, at_x, 0), net.pick(array, 1 - at_x, 0)
        came = net.send(theirs, net.to_x)
        first = at_x == 0
        return jnp.stack([jnp.where(first, mine, came), jnp.where(first, came, mine)])

    def to_home(array):
        mine = net.pick(array, at_x, 0)
        came = net.send(net.pick(array, 1 - at_x, 0), net.to_x)
        first = at_x == 0
        return jnp.stack([jnp.where(first, mine, came), jnp.where(first, came, mine)])

    def whole_row(array):
        other = net.send(array, net.to_core)
        return net.by_core(array, other, 1).reshape(ROW_LEN, array.shape[-1])

    def own_sum(array):
        view = array.reshape(2, 2, shard, array.shape[-1])
        came = net.send(net.pick(view, 1 - core, 1).astype(BF), net.to_core)
        return net.pick(view, core, 1) + came.astype(F32)

    lengths = net.pick(image_lengths, at_x, 0)
    widths = net.pick(grid_widths, at_x, 0)
    meta, segment = layout(lengths, widths)

    steps = jnp.arange(GRID)
    spread = (steps[:, None, None] - steps[None, :, None] + GRID - 1 == jnp.arange(SIDE)[None, None, :]).astype(BF)
    depth = -(-SIDE * GRID // 128) * 128
    cube = lax.dynamic_slice_in_dim(bias_table.reshape(SIDE, SIDE, heads), core * own_heads, own_heads, 2)
    tab = jnp.einsum("abh,ckb->hcak", cube, spread, preferred_element_type=F32).astype(BF)
    tab = jnp.pad(tab.reshape(own_heads * GRID, SIDE * GRID), ((0, 0), (0, depth - SIDE * GRID)))

    inputs = wide(to_own(tokens))
    upstream = wide(to_own(out_grad))

    normed, norm_one_pull = jax.vjp(norm_rows, inputs, gain_one, shift_one)
    h1 = whole_row(normed.astype(BF))
    joint = dot(h1, w_qkv)
    q = ((joint[:, :own_feats] + b_query) * scale).astype(BF)
    k = joint[:, own_feats : 2 * own_feats].astype(BF)
    v = (joint[:, 2 * own_feats :] + b_value).astype(BF)
    prob, mixed_heads = attn_fwd(meta, tab, q, k, v, segment)

    view = mixed_heads.reshape(2, 2, shard, own_feats)
    came = net.send(net.pick(view, 1 - core, 1), net.to_core)
    joined = net.by_core(net.pick(view, core, 1), came, 2).reshape(2 * shard, width)
    branch = (dot(joined, w_proj) + b_proj).reshape(2, shard, width)
    middle = inputs + layer_one * branch
    normed_two, norm_two_pull = jax.vjp(norm_rows, middle, gain_two, shift_two)
    h2 = whole_row(normed_two.astype(BF))
    before = dot(h2, w_up) + b_up
    activated, gelu_pull = jax.vjp(lambda hidden: jax.nn.gelu(hidden, approximate=False), before)
    act_low = activated.astype(BF)
    after = own_sum(dot(act_low, w_down)) + b_down
    mixed = to_home((middle + layer_two * after).astype(BF))

    d_layer_two = jnp.sum(upstream * after, axis=(0, 1))
    d_after_own = (layer_two * upstream).astype(BF)
    d_b_down = jnp.sum(wide(d_after_own), axis=(0, 1))
    d_after = whole_row(d_after_own)
    d_w_down = dot_t(act_low, d_after).astype(BF)
    g_down = net.reduce(d_w_down.reshape(dp, 2, rows_f, width))
    d_before = gelu_pull(dot_r(d_after, w_down))[0].astype(BF)
    d_b_up = jnp.sum(wide(d_before), axis=0)
    d_w_up = dot_t(h2, d_before).astype(BF)
    g_up = net.reduce(d_w_up.reshape(dp, 2, 2 * rows_w, ff // 2))
    d_h2 = own_sum(dot_r(d_before, w_up))
    d_middle_in, d_gain_two, d_shift_two = norm_two_pull(d_h2)
    d_middle = upstream + d_middle_in
    d_layer_one = jnp.sum(d_middle * branch, axis=(0, 1))
    d_branch = (layer_one * d_middle).astype(BF).reshape(2 * shard, width)
    d_b_proj = jnp.sum(wide(d_branch), axis=0)
    d_w_proj = dot_t(joined, d_branch).astype(BF)
    d_joined = dot_r(d_branch, w_proj).astype(BF).reshape(2, shard, 2, own_feats)
    came = net.send(net.pick(d_joined, 1 - core, 2), net.to_core)
    d_heads = net.by_core(net.pick(d_joined, core, 2), came, 1).reshape(ROW_LEN, own_feats)

    dq, dk, dv, grid = attn_bwd(meta, q, k, v, d_heads, prob, depth)
    grid = grid[:, : SIDE * GRID].reshape(own_heads, GRID, SIDE, GRID)
    table = jnp.einsum("hcak,ckb->hab", grid, wide(spread), precision=lax.Precision.HIGHEST)
    table = table.reshape(own_heads * SIDE * SIDE)
    pad = -table.shape[0] % 1024
    table_sum = net.total(jnp.pad(table, (0, pad)).reshape(-1, 128)).reshape(-1)[: table.shape[0]]
    table_sum = table_sum.reshape(own_heads, SIDE * SIDE)
    table_sum = net.by_core(table_sum, net.send(table_sum, net.to_core), 0).reshape(heads, SIDE * SIDE)
    table_grad = jnp.transpose(table_sum)

    dq_scaled = wide(dq) * scale
    d_b_query = jnp.sum(dq_scaled, axis=0)
    d_b_value = jnp.sum(wide(dv), axis=0)
    d_joint = jnp.concatenate([dq_scaled.astype(BF), dk, dv], axis=1)
    d_w_qkv = dot_t(h1, d_joint).astype(BF)
    g_qkv = net.reduce(d_w_qkv.reshape(dp, 2, 2 * rows_w, 3 * own_feats))
    d_h1 = own_sum(dot_r(d_joint, w_qkv))
    d_inputs_in, d_gain_one, d_shift_one = norm_one_pull(d_h1)
    tokens_grad = to_home((d_middle + d_inputs_in).astype(BF))

    def placed(part):
        return lax.dynamic_update_slice_in_dim(jnp.zeros((width,), F32), part, core * own_feats, 0)

    parts = [placed(d_b_query), placed(d_b_value), d_b_proj, d_b_down, d_gain_one, d_shift_one, d_gain_two, d_shift_two, d_layer_one, d_layer_two]
    parts = [a.reshape(dp, 2, 2, rows_w) for a in parts]
    up = d_b_up.reshape(dp, 2, 1, rows_f)
    mine = (jnp.arange(2) == core)[None, None, :, None]
    parts.append(jnp.where(mine, up, 0.0))
    parts = jnp.concatenate(parts, axis=-1).astype(BF)
    parts = jnp.pad(parts, ((0, 0), (0, 0), (0, 0), (0, width - n_small)))[:, :, :, None]
    fill = jnp.zeros((dp, 2, 2, pack_rows - rows_w - 1, width), BF)
    d_pack = jnp.concatenate([d_w_proj.reshape(dp, 2, 2, rows_w, width), parts, fill], axis=3)
    came = net.send(net.pick(d_pack, 1 - core, 2), net.to_core)
    g_pack = net.reduce((wide(net.pick(d_pack, core, 2)) + wide(came)).astype(BF))
    g_proj = g_pack[:rows_w]
    g_small = g_pack[rows_w, :n_small]
    smalls = [g_small[j * rows_w : (j + 1) * rows_w] for j in range(10)] + [g_small[10 * rows_w :]]

    def home(block, groups, cols):
        view = block.reshape(2, rows_w, groups, cols)
        came = net.send(net.pick(view, 1 - core, 0), net.to_core)
        return net.by_core(net.pick(view, core, 0), came, 2).reshape(rows_w, groups * 2 * cols)

    g_qkv = home(g_qkv, 3, own_feats)
    g_up = home(g_up, chips, rows_f)
    g_query, g_value, g_bproj, g_bdown, g_gain1, g_shift1, g_gain2, g_shift2, g_layer1, g_layer2, g_bup = smalls
    return (
        mixed,
        tokens_grad,
        g_qkv,
        g_query,
        g_value,
        g_proj,
        g_bproj,
        g_up,
        g_bup,
        g_down,
        g_bdown,
        g_gain1,
        g_shift1,
        g_gain2,
        g_shift2,
        g_layer1,
        g_layer2,
        table_grad,
    )


def solution(mesh):
    both = P(BOTH)
    both2 = P(BOTH, None)
    act = P("dp", "seq", None)
    in_specs = (act, P("dp", None), P("dp", None), both2, both, both, both2, both, both2, both, both2)
    in_specs += (both,) * 7 + (P(), act)
    out_specs = (act, act, both2, both, both, both2, both, both2, both, both2) + (both,) * 7 + (P(),)
    body = functools.partial(local, mesh.shape["dp"], mesh.shape["seq"])
    return jax.shard_map(body, mesh=mesh, in_specs=in_specs, out_specs=out_specs, check_vma=False)
```

time: 1280 us -> 398 us (0.31)
  waiting for transfers between devices: 574 us -> 82.3 us
  matrix products: 406 us -> 36 us
  starting transfers between devices: 1.07 us -> 90.6 us
  blocking collectives: 82.9 us -> 0 us
  Pallas kernels: 0 us -> 71 us
  other arithmetic: 125 us -> 54.6 us
  local copies, waits for them, and re-layouts: 70.2 us -> 56.7 us
    reduce_scatter x6 -> x0, waiting for transfers between devices: 515 us -> none  [the longest x1 142 us: local(): lax.psum_scatter(grad_w_up, ('dp', 'seq'), scatter_dimension=0, tiled=True)]
    dot_general x42 -> x14, matrix products: 406 us -> 36 us  [the longest x4 16.3 us: dot_r(): lax.dot_general(a, b, (((1,), (1,)), ((), ())), preferred_element_type=F32)]
    dot_general x12 -> x0, other arithmetic: 102 us -> none  [table_sum(): jnp.einsum('rqka,rqkb->ab', rows_hot, weighted, preferred_element_type=jn...]
    ppermute x0 -> x55, starting transfers between devices: none -> 90.6 us  [send(): return lax.ppermute(array, BOTH, pairs)]
    unnamed x2 -> x0, blocking collectives: 82.9 us -> none
    ppermute x0 -> x55, waiting for transfers between devices: none -> 82.3 us  [send(): return lax.ppermute(array, BOTH, pairs)]
    pallas_call x0 -> x10, Pallas kernels: none -> 71 us  [the longest x1 34.3 us: attn_bwd(): pl.pallas_call(attn_bwd_kernel, out_shape=(low, low, low, jax.ShapeDtypeS...]
    psum x1 -> x0, waiting for transfers between devices: 46.2 us -> none  [local(): table_total = lax.psum(grad_table, ('dp', 'seq'))]
  transfers between devices with their start and end apart: 13 -> 55, of which waited for: 6 -> 18; matrix products, arithmetic and copies ran while one was open for 43% -> 28% of each run, Pallas kernels for 0% -> 18%
where the time goes in v1:
time: 398 us; the launch traced here: 394 us
  starting transfers between devices  90.6 us (23%)
  waiting for transfers between devices  82.3 us (21%)
  Pallas kernels  71 us (18%)
  local copies, waits for them, and re-layouts  56.7 us (14%)
  other arithmetic  54.6 us (14%)
  matrix products  36 us (9%)
    ppermute x55, starting transfers between devices, send(): return lax.ppermute(array, BOTH, pairs)  90.6 us
    ppermute x55, waiting for transfers between devices, send(): return lax.ppermute(array, BOTH, pairs)  82.3 us
    pallas_call x1, Pallas kernels, attn_bwd(): pl.pallas_call(attn_bwd_kernel, out_shape=(low, low, low, jax.ShapeDtypeS...  34.3 us
    pallas_call x1, Pallas kernels, attn_fwd(): pl.pallas_call(attn_fwd_kernel, out_shape=(jax.ShapeDtypeStruct((heads, R...  31.3 us
    dot_general x4, matrix products, dot_r(): lax.dot_general(a, b, (((1,), (1,)), ((), ())), preferred_element_type=F32)  16.3 us
    another operation x17, other arithmetic, gather(): block = jnp.stack([block, self.send(block, pairs)])  13.5 us
    dot_general x4, matrix products, dot_t(): lax.dot_general(a, b, (((0,), (0,)), ((), ())), preferred_element_type=F32)  10.6 us
  transfers between devices with their start and end apart: 55, of which 18 were waited for; matrix products, arithmetic and copies ran while one was open for 28% of the time, Pallas kernels for 18%

profile of v1, /device:TPU:0, one launch (start us, length us, event | category | flops | bytes accessed | tf_op | source)
XLA Modules:
  0.0 394.3 jit_solution(16798901154375115665)
XLA Ops:
  0.7 7.5 %concatenate.28 = bf16[336]{0:T(512)(128)(2,1)S(1)} concatenate(bf16[24]{0:T(256)(128)(2,1)} %param.24, bf16[24]{0:T(256)(128)(2,1)} %param.25, bf16[24]{0:T(256)(128)(2,1)} %param.27, bf16[24]{0:T(256)(128)(2,1)} %param.31, bf16[24]{0:T(256)(128)(2,1)} %param.32, bf16[24]{0:T(256)(128)(2,1)} %param.33, bf16[24]{0:T(256)(128)(2,1)} %param.34, bf16[24]{0:T(256)(128)(2,1)} %param.35, ...), dimensions={0} | concatenate | bytes 1344 | tf_op jit(solution)/shard_map/concatenate | solution.py:415
  9.8 4.0 %collective-permute-start.1 = (bf16[32,768]{1,0:T(8,128)(2,1)}, bf16[32,768]{1,0:T(8,128)(2,1)}, u32[]{:S(2)}, u32[]{:S(2)}) collective-permute-start(bf16[32,768]{1,0:T(8,128)(2,1)} %get-tuple-element.131), channel_id=1, source_target_pairs={{0,16},{1,17},{2,18},{3,19},{4,20},{5,21},{6,22},{7,23},{8,24},{9,... | collective-permute-start | bytes 147464 | tf_op jit(solution)/shard_map/ppermute | solution.py:317
  31.5 2.7 collective-permute-start.8
  39.7 3.6 collective-permute-done.8
  49.7 8.2 %collective-permute-done.9 = bf16[2,48,1152]{2,1,0:T(8,128)(2,1)S(1)} collective-permute-done((bf16[2,48,1152]{2,1,0:T(8,128)(2,1)S(1)}, bf16[2,48,1152]{2,1,0:T(8,128)(2,1)S(1)}, u32[]{:S(2)}, u32[]{:S(2)}) %collective-permute-start.9) | collective-permute-done | bytes 221216 | tf_op jit(solution)/shard_map/ppermute | solution.py:317
  60.3 2.6 collective-permute-done.16
  69.4 5.6 %collective-permute-done.21 = bf16[2,2,96,768]{3,2,1,0:T(8,128)(2,1)S(1)} collective-permute-done((bf16[2,2,96,768]{3,2,1,0:T(8,128)(2,1)S(1)}, bf16[2,2,96,768]{3,2,1,0:T(8,128)(2,1)S(1)}, u32[]{:S(2)}, u32[]{:S(2)}) %collective-permute-start.21) | collective-permute-done | bytes 589856 | tf_op jit(solution)/shard_map/ppermute | solution.py:317
  78.1 9.5 %collective-permute-done.17 = bf16[2,2,48,1536]{3,2,1,0:T(8,128)(2,1)S(1)} collective-permute-done((bf16[2,2,48,1536]{3,2,1,0:T(8,128)(2,1)S(1)}, bf16[2,2,48,1536]{3,2,1,0:T(8,128)(2,1)S(1)}, u32[]{:S(2)}, u32[]{:S(2)}) %collective-permute-start.17) | collective-permute-done | bytes 589856 | tf_op jit(solution)/shard_map/ppermute | solution.py:317
  103.9 31.3 %attn_fwd.1 = (bf16[6,576,576]{2,1,0:T(8,128)(2,1)}, bf16[576,384]{1,0:T(8,128)(2,1)S(1)}) custom-call(s32[4,5]{1,0:T(4,128)S(1)} %pad_add_fusion.meta, bf16[144,1152]{1,0:T(8,128)(2,1)S(1)} %pad.17.tab, bf16[576,384]{1,0:T(8,128)(2,1)S(1)} %get-tuple-element.52.q, bf16[576,384]{1,0:T(8,128)(2,1)S(1)} %slice.457.k, ...), custom_call_target="tpu_custom_call" | custom-call | flops 2000000000 | bytes 8000000 | tf_op jit(solution)/shard_map/attn_fwd/pallas_call | solution.py:223
  147.8 10.6 %convert_reduce_fusion = (bf16[1536]{0:T(1024)(128)(2,1)S(1)}, bf16[576,1536]{1,0:T(8,128)(2,1)}, f32[576,1536]{1,0:T(8,128)S(1)}) fusion(f32[576,1536]{1,0:T(8,128)S(1)} %convolution_add_fusion, bf16[576,768]{1,0:T(8,128)(2,1)S(1)} %bitcast.427, bf16[1536,768]{1,0:T(8,128)(2,1)S(1)} %bitcast.398), kind=kOutput, calls=%fused_computation.2 | convolution fusion | flops 1424423424 | bytes 12094464 | tf_op jit(solution)/shard_map/dot_general | solution.py:374
  160.6 3.9 convolution_convert_fusion
  183.9 2.7 convolution_convert_fusion.5
  190.1 2.8 constant_dynamic-slice_fusion.3
  193.7 3.1 fusion.9
  200.6 2.8 collective-permute-start.24
  203.5 3.0 convolution_convert_fusion.3
  207.6 34.3 %attn_bwd.1 = (bf16[576,384]{1,0:T(8,128)(2,1)S(1)}, bf16[576,384]{1,0:T(8,128)(2,1)S(1)}, bf16[576,384]{1,0:T(8,128)(2,1)S(1)}, f32[144,1152]{1,0:T(8,128)S(1)}) custom-call(s32[4,5]{1,0:T(4,128)S(1)} %pad_add_fusion.meta, bf16[576,384]{1,0:T(8,128)(2,1)S(1)} %copy-done.15, bf16[576,384]{1,0:T(8,128)(2,1)S(1)} %copy-done.11, ...), custom_call_target="tpu_custom_call" | custom-call | flops 5000000000 | bytes 8000000 | tf_op jit(solution)/shard_map/attn_bwd/pallas_call | solution.py:244
  243.4 3.4 reshape.524
  246.8 3.7 convolution_bitcast_fusion
  250.7 31.4 %collective-permute-start.50 = (f32[104,128]{1,0:T(8,128)S(1)}, f32[104,128]{1,0:T(8,128)S(1)}, u32[]{:S(2)}, u32[]{:S(2)}) collective-permute-start(f32[104,128]{1,0:T(8,128)S(1)} %pad_bitcast_fusion), channel_id=1, source_target_pairs={{0,16},{1,17},{2,18},{3,19},{4,20},{5,21},{6,22},{7,23},{8,24},{9,... | collective-permute-start | bytes 159752 | tf_op jit(solution)/shard_map/ppermute | solution.py:317
  286.4 3.0 collective-permute-start.51
  293.3 7.7 %collective-permute-start.29 = (bf16[2,144,768]{2,1,0:T(8,128)(2,1)}, bf16[2,144,768]{2,1,0:T(8,128)(2,1)}, u32[]{:S(2)}, u32[]{:S(2)}) collective-permute-start(bf16[2,144,768]{2,1,0:T(8,128)(2,1)} %fusion.18), channel_id=1, source_target_pairs={{0,1},{1,0},{2,3},{3,2},{4,5},{5,4},{6,7},{7,6},{8,9},{9,8},{10,11... | collective-permute-start | bytes 1327112 | tf_op jit(solution)/shard_map/ppermute | solution.py:317
  302.1 2.7 collective-permute-start.31
  305.8 10.7 %collective-permute-done.53 = f32[104,128]{1,0:T(8,128)S(1)} collective-permute-done((f32[104,128]{1,0:T(8,128)S(1)}, f32[104,128]{1,0:T(8,128)S(1)}, u32[]{:S(2)}, u32[]{:S(2)}) %collective-permute-start.53) | collective-permute-done | bytes 53280 | tf_op jit(solution)/shard_map/ppermute | solution.py:317
  319.2 2.5 fusion.79
  340.4 6.0 %collective-permute-done.42 = bf16[4,48,1536]{2,1,0:T(8,128)(2,1)S(1)} collective-permute-done((bf16[4,48,1536]{2,1,0:T(8,128)(2,1)S(1)}, bf16[4,48,1536]{2,1,0:T(8,128)(2,1)S(1)}, u32[]{:S(2)}, u32[]{:S(2)}) %collective-permute-start.42) | collective-permute-done | bytes 589856 | tf_op jit(solution)/shard_map/ppermute | solution.py:317
  349.7 2.7 collective-permute-done.32
  352.6 3.9 collective-permute-done.43
  360.4 8.2 %collective-permute-done.44 = bf16[1,48,1536]{2,1,0:T(8,128)(2,1)S(1)} collective-permute-done((bf16[1,48,1536]{2,1,0:T(8,128)(2,1)S(1)}, bf16[1,48,1536]{2,1,0:T(8,128)(2,1)S(1)}, u32[]{:S(2)}, u32[]{:S(2)}) %collective-permute-start.44) | collective-permute-done | bytes 147488 | tf_op jit(solution)/shard_map/ppermute | solution.py:317
  372.5 6.1 %collective-permute-done.34 = bf16[1,48,1152]{2,1,0:T(8,128)(2,1)S(1)} collective-permute-done((bf16[1,48,1152]{2,1,0:T(8,128)(2,1)S(1)}, bf16[1,48,1152]{2,1,0:T(8,128)(2,1)S(1)}, u32[]{:S(2)}, u32[]{:S(2)}) %collective-permute-start.34) | collective-permute-done | bytes 110624 | tf_op jit(solution)/shard_map/ppermute | solution.py:317
  381.7 5.1 %collective-permute-done.39 = bf16[2,32,768]{2,1,0:T(8,128)(2,1)S(1)} collective-permute-done((bf16[2,32,768]{2,1,0:T(8,128)(2,1)S(1)}, bf16[2,32,768]{2,1,0:T(8,128)(2,1)S(1)}, u32[]{:S(2)}, u32[]{:S(2)}) %collective-permute-start.39) | collective-permute-done | bytes 98336 | tf_op jit(solution)/shard_map/ppermute | solution.py:317
  388.8 3.4 collective-permute-done.40
  (481 shorter events, 152.5 us)
Async XLA Ops:
  9.8 17.6 %collective-permute-start.1 = (bf16[32,768]{1,0:T(8,128)(2,1)}, bf16[32,768]{1,0:T(8,128)(2,1)}, u32[]{:S(2)}, u32[]{:S(2)}) collective-permute-start(bf16[32,768]{1,0:T(8,128)(2,1)} %get-tuple-element.131), channel_id=1, source_target_pairs={{0,16},{1,17},{2,18},{3,19},{4,20},{5,21},{6,22},{7,23},{8,24},{9,... | collective-permute-start | bytes 147464 | tf_op jit(solution)/shard_map/ppermute | solution.py:317
  15.7 13.1 %collective-permute-start.7 = (bf16[24,3,384]{2,0,1:T(8,128)(2,1)}, bf16[24,3,384]{2,0,1:T(8,128)(2,1)}, u32[]{:S(2)}, u32[]{:S(2)}) collective-permute-start(bf16[24,3,384]{2,0,1:T(8,128)(2,1)} %bitcast.388), channel_id=1, source_target_pairs={{0,1},{1,0},{2,3},{3,2},{4,5},{5,4},{6,7},{7,6},{8,9},{9,8},{10,11... | collective-permute-start | bytes 165896 | tf_op jit(solution)/shard_map/ppermute | solution.py:317
  15.7 21.5 %collective-permute-start.19 = (bf16[96,768]{1,0:T(8,128)(2,1)}, bf16[96,768]{1,0:T(8,128)(2,1)}, u32[]{:S(2)}, u32[]{:S(2)}) collective-permute-start(bf16[96,768]{1,0:T(8,128)(2,1)} %param.30), channel_id=1, source_target_pairs={{0,16},{1,17},{2,18},{3,19},{4,20},{5,21},{6,22},{7,23},{8,24},{9,... | collective-permute-start | bytes 442376 | tf_op jit(solution)/shard_map/ppermute | solution.py:317
  17.9 13.6 %collective-permute-start.14 = (bf16[24,16,96]{2,1,0:T(8,128)(2,1)}, bf16[24,16,96]{2,1,0:T(8,128)(2,1)}, u32[]{:S(2)}, u32[]{:S(2)}) collective-permute-start(bf16[24,16,96]{2,1,0:T(8,128)(2,1)} %bitcast.387), channel_id=1, source_target_pairs={{0,1},{1,0},{2,3},{3,2},{4,5},{5,4},{6,7},{7,6},{8,9},{9,8},{10,11... | collective-permute-start | bytes 221192 | tf_op jit(solution)/shard_map/ppermute | solution.py:317
  18.4 28.6 %collective-permute-start.25 = (bf16[144,768]{1,0:T(8,128)(2,1)S(1)}, bf16[144,768]{1,0:T(8,128)(2,1)}, u32[]{:S(2)}, u32[]{:S(2)}) collective-permute-start(bf16[144,768]{1,0:T(8,128)(2,1)S(1)} %dynamic-slice_bitcast_fusion.2), channel_id=1, source_target_pairs={{0,2},{1,3},{2,0},{3,1},{4,6},{5,7},{6,4},{7,5},{8,10},{9,11},{10,... | collective-permute-start | bytes 663560 | tf_op jit(solution)/shard_map/ppermute | solution.py:317
  27.4 16.9 %collective-permute-start = (bf16[144,768]{1,0:T(8,128)(2,1)}, bf16[144,768]{1,0:T(8,128)(2,1)S(1)}, u32[]{:S(2)}, u32[]{:S(2)}) collective-permute-start(bf16[144,768]{1,0:T(8,128)(2,1)} %dynamic-slice_bitcast_fusion.5), channel_id=1, source_target_pairs={{0,2},{1,3},{2,0},{3,1},{4,6},{5,7},{6,4},{7,5},{8,10},{9,11},{10,... | collective-permute-start | bytes 663560 | tf_op jit(solution)/shard_map/ppermute | solution.py:317
  43.3 16.4 %collective-permute-start.20 = (bf16[2,96,768]{2,1,0:T(8,128)(2,1)S(1)}, bf16[2,96,768]{2,1,0:T(8,128)(2,1)S(1)}, u32[]{:S(2)}, u32[]{:S(2)}) collective-permute-start(bf16[2,96,768]{2,1,0:T(8,128)(2,1)S(1)} %get-tuple-element.101), channel_id=1, source_target_pairs={{0,8},{1,9},{2,10},{3,11},{4,12},{5,13},{6,14},{7,15},{8,0},{9,1},... | collective-permute-start | bytes 884744 | tf_op jit(solution)/shard_map/ppermute | solution.py:317
  44.2 13.7 %collective-permute-start.9 = (bf16[2,48,1152]{2,1,0:T(8,128)(2,1)S(1)}, bf16[2,48,1152]{2,1,0:T(8,128)(2,1)S(1)}, u32[]{:S(2)}, u32[]{:S(2)}) collective-permute-start(bf16[2,48,1152]{2,1,0:T(8,128)(2,1)S(1)} %get-tuple-element.105), channel_id=1, source_target_pairs={{0,8},{1,9},{2,10},{3,11},{4,12},{5,13},{6,14},{7,15},{8,0},{9,1},... | collective-permute-start | bytes 663560 | tf_op jit(solution)/shard_map/ppermute | solution.py:317
  46.6 16.2 %collective-permute-start.16 = (bf16[2,48,1536]{2,1,0:T(8,128)(2,1)S(1)}, bf16[2,48,1536]{2,1,0:T(8,128)(2,1)S(1)}, u32[]{:S(2)}, u32[]{:S(2)}) collective-permute-start(bf16[2,48,1536]{2,1,0:T(8,128)(2,1)S(1)} %get-tuple-element.97), channel_id=1, source_target_pairs={{0,8},{1,9},{2,10},{3,11},{4,12},{5,13},{6,14},{7,15},{8,0},{9,1},... | collective-permute-start | bytes 884744 | tf_op jit(solution)/shard_map/ppermute | solution.py:317
  48.1 16.4 %collective-permute-start.4 = (bf16[2,2,2,32,768]{4,3,2,1,0:T(8,128)(2,1)S(1)}, bf16[2,2,2,32,768]{4,3,2,1,0:T(8,128)(2,1)S(1)}, u32[]{:S(2)}, u32[]{:S(2)}) collective-permute-start(bf16[2,2,2,32,768]{4,3,2,1,0:T(8,128)(2,1)S(1)} %get-tuple-element.93), channel_id=1, source_target_pairs={{0,4},{1,3},{2,6},{3,1},{4,0},{5,7},{6,2},{7,5},{8,12},{9,11},{10,... | collective-permute-start | bytes 1179656 | tf_op jit(solution)/shard_map/ppermute | solution.py:317
  59.7 15.3 %collective-permute-start.21 = (bf16[2,2,96,768]{3,2,1,0:T(8,128)(2,1)S(1)}, bf16[2,2,96,768]{3,2,1,0:T(8,128)(2,1)S(1)}, u32[]{:S(2)}, u32[]{:S(2)}) collective-permute-start(bf16[2,2,96,768]{3,2,1,0:T(8,128)(2,1)S(1)} %get-tuple-element.85), channel_id=1, source_target_pairs={{0,2},{1,5},{2,0},{3,7},{4,6},{5,1},{6,4},{7,3},{8,10},{9,13},{10,... | collective-permute-start | bytes 1769480 | tf_op jit(solution)/shard_map/ppermute | solution.py:317
  62.9 24.7 %collective-permute-start.17 = (bf16[2,2,48,1536]{3,2,1,0:T(8,128)(2,1)S(1)}, bf16[2,2,48,1536]{3,2,1,0:T(8,128)(2,1)S(1)}, u32[]{:S(2)}, u32[]{:S(2)}) collective-permute-start(bf16[2,2,48,1536]{3,2,1,0:T(8,128)(2,1)S(1)} %get-tuple-element.83), channel_id=1, source_target_pairs={{0,2},{1,5},{2,0},{3,7},{4,6},{5,1},{6,4},{7,3},{8,10},{9,13},{10,... | collective-permute-start | bytes 1769480 | tf_op jit(solution)/shard_map/ppermute | solution.py:317
  65.6 25.0 %collective-permute-start.5 = (bf16[8,2,32,768]{3,0,2,1:T(8,128)(2,1)S(1)}, bf16[8,2,32,768]{3,0,2,1:T(8,128)(2,1)S(1)}, u32[]{:S(2)}, u32[]{:S(2)}) collective-permute-start(bf16[8,2,32,768]{3,0,2,1:T(8,128)(2,1)S(1)} %copy.141), channel_id=1, source_target_pairs={{0,1},{1,0},{2,3},{3,2},{4,5},{5,4},{6,7},{7,6},{8,9},{9,8},{10,11... | collective-permute-start | bytes 2359304 | tf_op jit(solution)/shard_map/ppermute | solution.py:317
  67.8 30.6 %collective-permute-start.11 = (bf16[2,2,2,48,1152]{4,3,2,1,0:T(8,128)(2,1)}, bf16[2,2,2,48,1152]{4,3,2,1,0:T(8,128)(2,1)}, u32[]{:S(2)}, u32[]{:S(2)}) collective-permute-start(bf16[2,2,2,48,1152]{4,3,2,1,0:T(8,128)(2,1)} %get-tuple-element.65), channel_id=1, source_target_pairs={{0,4},{1,3},{2,6},{3,1},{4,0},{5,7},{6,2},{7,5},{8,12},{9,11},{10,... | collective-permute-start | bytes 2654216 | tf_op jit(solution)/shard_map/ppermute | solution.py:317
  76.6 62.6 %collective-permute-start.22 = (bf16[2,2,2,96,768]{4,3,2,1,0:T(8,128)(2,1)}, bf16[2,2,2,96,768]{4,3,2,1,0:T(8,128)(2,1)}, u32[]{:S(2)}, u32[]{:S(2)}) collective-permute-start(bf16[2,2,2,96,768]{4,3,2,1,0:T(8,128)(2,1)} %get-tuple-element.59), channel_id=1, source_target_pairs={{0,4},{1,3},{2,6},{3,1},{4,0},{5,7},{6,2},{7,5},{8,12},{9,11},{10,... | collective-permute-start | bytes 3538952 | tf_op jit(solution)/shard_map/ppermute | solution.py:317
  89.2 52.9 %collective-permute-start.18 = (bf16[2,2,2,48,1536]{4,3,2,1,0:T(8,128)(2,1)}, bf16[2,2,2,48,1536]{4,3,2,1,0:T(8,128)(2,1)}, u32[]{:S(2)}, u32[]{:S(2)}) collective-permute-start(bf16[2,2,2,48,1536]{4,3,2,1,0:T(8,128)(2,1)} %get-tuple-element.57), channel_id=1, source_target_pairs={{0,4},{1,3},{2,6},{3,1},{4,0},{5,7},{6,2},{7,5},{8,12},{9,11},{10,... | collective-permute-start | bytes 3538952 | tf_op jit(solution)/shard_map/ppermute | solution.py:317
  97.8 37.6 %collective-permute-start.26 = (bf16[2,144,768]{2,1,0:T(8,128)(2,1)}, bf16[2,144,768]{2,1,0:T(8,128)(2,1)S(1)}, u32[]{:S(2)}, u32[]{:S(2)}) collective-permute-start(bf16[2,144,768]{2,1,0:T(8,128)(2,1)} %get-tuple-element.43), channel_id=1, source_target_pairs={{0,1},{1,0},{2,3},{3,2},{4,5},{5,4},{6,7},{7,6},{8,9},{9,8},{10,11... | collective-permute-start | bytes 1327112 | tf_op jit(solution)/shard_map/ppermute | solution.py:317
  169.4 24.2 %collective-permute-start.23 = (bf16[2,144,768]{2,1,0:T(8,128)(2,1)}, bf16[2,144,768]{2,1,0:T(8,128)(2,1)}, u32[]{:S(2)}, u32[]{:S(2)}) collective-permute-start(bf16[2,144,768]{2,1,0:T(8,128)(2,1)} %fusion.16), channel_id=1, source_target_pairs={{0,1},{1,0},{2,3},{3,2},{4,5},{5,4},{6,7},{7,6},{8,9},{9,8},{10,11... | collective-permute-start | bytes 1327112 | tf_op jit(solution)/shard_map/ppermute | solution.py:317
  172.8 155.6 %collective-permute-start.46 = (bf16[8,96,768]{2,1,0:T(8,128)(2,1)}, bf16[8,96,768]{2,1,0:T(8,128)(2,1)}, u32[]{:S(2)}, u32[]{:S(2)}) collective-permute-start(bf16[8,96,768]{2,1,0:T(8,128)(2,1)} %slice.393), channel_id=1, source_target_pairs={{0,4},{1,3},{2,6},{3,1},{4,0},{5,7},{6,2},{7,5},{8,12},{9,11},{10,... | collective-permute-start | bytes 3538952 | tf_op jit(solution)/shard_map/ppermute | solution.py:317
  176.7 154.1 %collective-permute-start.41 = (bf16[8,48,1536]{2,1,0:T(8,128)(2,1)}, bf16[8,48,1536]{2,1,0:T(8,128)(2,1)}, u32[]{:S(2)}, u32[]{:S(2)}) collective-permute-start(bf16[8,48,1536]{2,1,0:T(8,128)(2,1)} %slice.384), channel_id=1, source_target_pairs={{0,4},{1,3},{2,6},{3,1},{4,0},{5,7},{6,2},{7,5},{8,12},{9,11},{10,... | collective-permute-start | bytes 3538952 | tf_op jit(solution)/shard_map/ppermute | solution.py:317
  193.6 12.8 %collective-permute-start.28 = (bf16[2,144,384]{2,1,0:T(8,128)(2,1)}, bf16[2,144,384]{2,1,0:T(8,128)(2,1)}, u32[]{:S(2)}, u32[]{:S(2)}) collective-permute-start(bf16[2,144,384]{2,1,0:T(8,128)(2,1)} %bitcast.385), channel_id=1, source_target_pairs={{0,1},{1,0},{2,3},{3,2},{4,5},{5,4},{6,7},{7,6},{8,9},{9,8},{10,11... | collective-permute-start | bytes 663560 | tf_op jit(solution)/shard_map/ppermute | solution.py:317
  200.6 104.1 %collective-permute-start.24 = (bf16[144,768]{1,0:T(8,128)(2,1)}, bf16[144,768]{1,0:T(8,128)(2,1)}, u32[]{:S(2)}, u32[]{:S(2)}) collective-permute-start(bf16[144,768]{1,0:T(8,128)(2,1)} %dynamic-slice_bitcast_fusion.3), channel_id=1, source_target_pairs={{0,2},{1,3},{2,0},{3,1},{4,6},{5,7},{6,4},{7,5},{8,10},{9,11},{10,... | collective-permute-start | bytes 663560 | tf_op jit(solution)/shard_map/ppermute | solution.py:317
  250.7 35.7 %collective-permute-start.50 = (f32[104,128]{1,0:T(8,128)S(1)}, f32[104,128]{1,0:T(8,128)S(1)}, u32[]{:S(2)}, u32[]{:S(2)}) collective-permute-start(f32[104,128]{1,0:T(8,128)S(1)} %pad_bitcast_fusion), channel_id=1, source_target_pairs={{0,16},{1,17},{2,18},{3,19},{4,20},{5,21},{6,22},{7,23},{8,24},{9,... | collective-permute-start | bytes 159752 | tf_op jit(solution)/shard_map/ppermute | solution.py:317
  293.3 25.9 %collective-permute-start.29 = (bf16[2,144,768]{2,1,0:T(8,128)(2,1)}, bf16[2,144,768]{2,1,0:T(8,128)(2,1)}, u32[]{:S(2)}, u32[]{:S(2)}) collective-permute-start(bf16[2,144,768]{2,1,0:T(8,128)(2,1)} %fusion.18), channel_id=1, source_target_pairs={{0,1},{1,0},{2,3},{3,2},{4,5},{5,4},{6,7},{7,6},{8,9},{9,8},{10,11... | collective-permute-start | bytes 1327112 | tf_op jit(solution)/shard_map/ppermute | solution.py:317
  302.1 32.6 %collective-permute-start.31 = (bf16[8,48,1152]{2,1,0:T(8,128)(2,1)}, bf16[8,48,1152]{2,1,0:T(8,128)(2,1)}, u32[]{:S(2)}, u32[]{:S(2)}) collective-permute-start(bf16[8,48,1152]{2,1,0:T(8,128)(2,1)} %slice.364), channel_id=1, source_target_pairs={{0,4},{1,3},{2,6},{3,1},{4,0},{5,7},{6,2},{7,5},{8,12},{9,11},{10,... | collective-permute-start | bytes 2654216 | tf_op jit(solution)/shard_map/ppermute | solution.py:317
  328.1 18.6 %collective-permute-start.36 = (bf16[8,2,32,768]{3,2,1,0:T(8,128)(2,1)S(1)}, bf16[8,2,32,768]{3,2,1,0:T(8,128)(2,1)S(1)}, u32[]{:S(2)}, u32[]{:S(2)}) collective-permute-start(bf16[8,2,32,768]{3,2,1,0:T(8,128)(2,1)S(1)} %dynamic-slice_bitcast_fusion), channel_id=1, source_target_pairs={{0,1},{1,0},{2,3},{3,2},{4,5},{5,4},{6,7},{7,6},{8,9},{9,8},{10,11... | collective-permute-start | bytes 2359304 | tf_op jit(solution)/shard_map/ppermute | solution.py:317
  332.4 14.0 %collective-permute-start.42 = (bf16[4,48,1536]{2,1,0:T(8,128)(2,1)S(1)}, bf16[4,48,1536]{2,1,0:T(8,128)(2,1)S(1)}, u32[]{:S(2)}, u32[]{:S(2)}) collective-permute-start(bf16[4,48,1536]{2,1,0:T(8,128)(2,1)S(1)} %slice.386), channel_id=1, source_target_pairs={{0,2},{1,5},{2,0},{3,7},{4,6},{5,1},{6,4},{7,3},{8,10},{9,13},{10,... | collective-permute-start | bytes 1769480 | tf_op jit(solution)/shard_map/ppermute | solution.py:317
  336.1 16.3 %collective-permute-start.32 = (bf16[4,48,1152]{2,1,0:T(8,128)(2,1)S(1)}, bf16[4,48,1152]{2,1,0:T(8,128)(2,1)S(1)}, u32[]{:S(2)}, u32[]{:S(2)}) collective-permute-start(bf16[4,48,1152]{2,1,0:T(8,128)(2,1)S(1)} %slice.366), channel_id=1, source_target_pairs={{0,2},{1,5},{2,0},{3,7},{4,6},{5,1},{6,4},{7,3},{8,10},{9,13},{10,... | collective-permute-start | bytes 1327112 | tf_op jit(solution)/shard_map/ppermute | solution.py:317
  340.3 17.4 %collective-permute-start.48 = (bf16[2,96,768]{2,1,0:T(8,128)(2,1)S(1)}, bf16[2,96,768]{2,1,0:T(8,128)(2,1)S(1)}, u32[]{:S(2)}, u32[]{:S(2)}) collective-permute-start(bf16[2,96,768]{2,1,0:T(8,128)(2,1)S(1)} %slice.397), channel_id=1, source_target_pairs={{0,8},{1,9},{2,10},{3,11},{4,12},{5,13},{6,14},{7,15},{8,0},{9,1},... | collective-permute-start | bytes 884744 | tf_op jit(solution)/shard_map/ppermute | solution.py:317
  347.6 24.5 %collective-permute-start.37 = (bf16[8,32,768]{2,1,0:T(8,128)(2,1)S(1)}, bf16[8,32,768]{2,1,0:T(8,128)(2,1)S(1)}, u32[]{:S(2)}, u32[]{:S(2)}) collective-permute-start(bf16[8,32,768]{2,1,0:T(8,128)(2,1)S(1)} %slice.372), channel_id=1, source_target_pairs={{0,4},{1,3},{2,6},{3,1},{4,0},{5,7},{6,2},{7,5},{8,12},{9,11},{10,... | collective-permute-start | bytes 1179656 | tf_op jit(solution)/shard_map/ppermute | solution.py:317
  352.6 19.4 %collective-permute-start.33 = (bf16[2,48,1152]{2,1,0:T(8,128)(2,1)S(1)}, bf16[2,48,1152]{2,1,0:T(8,128)(2,1)S(1)}, u32[]{:S(2)}, u32[]{:S(2)}) collective-permute-start(bf16[2,48,1152]{2,1,0:T(8,128)(2,1)S(1)} %slice.368), channel_id=1, source_target_pairs={{0,8},{1,9},{2,10},{3,11},{4,12},{5,13},{6,14},{7,15},{8,0},{9,1},... | collective-permute-start | bytes 663560 | tf_op jit(solution)/shard_map/ppermute | solution.py:317
  356.7 12.0 %collective-permute-start.44 = (bf16[1,48,1536]{2,1,0:T(8,128)(2,1)S(1)}, bf16[1,48,1536]{2,1,0:T(8,128)(2,1)S(1)}, u32[]{:S(2)}, u32[]{:S(2)}) collective-permute-start(bf16[1,48,1536]{2,1,0:T(8,128)(2,1)S(1)} %slice.390), channel_id=1, source_target_pairs={{0,16},{1,17},{2,18},{3,19},{4,20},{5,21},{6,22},{7,23},{8,24},{9,... | collective-permute-start | bytes 442376 | tf_op jit(solution)/shard_map/ppermute | solution.py:317
  (91 other events, 1212.3 us)
